TPU v7x, 32 devices: a whole 2x2x4 slice. The times are simulated.
32 devices in a mesh: doc: 16 (over z, y, x), qry: 2 (over core).
Axes of the slice: x: 2, y: 2, z: 4, core: 2. Of those that a mesh axis runs over, the one named last changes fastest.
Arguments:
- queries: bfloat16 [64, 4096], P('qry'), may hold values from -14 to 14
- passages: bfloat16 [4352, 4096], P(('doc', 'qry')), may hold values from -14 to 14
- passage_route: int32 [4352], P(('doc', 'qry')), may hold values from 0 to 8191, as said below
- pattern: int32 [2, 32], replicated, may hold values from 0 to 1, as said below
- teacher: float32 [64, 512], P(None, ('doc', 'qry')), may hold values from -20 to 270
Outputs:
- doc_scores: float32 [64, 512], P(None, ('doc', 'qry'))
- divergence: float32 [64], P('qry')
Inputs may be any that keep to these rules, and one draw needn't show every extreme that they name: `passage_route`: A value v names document v // 16 (device g owns documents g * 16 to g * 16 + 15, with g = doc index * 2 + qry index) and passage v % 16 of it. Every document has 1 to 16 passages numbered from 0 without gaps, each held once over all shards, and its owner has the qry index of the shards that hold them. The passages of one owner are spread over the 16 shards of that qry index as evenly as possible (counts differ by at most one), so at most 16 go from one shard to one owner; in every qry index one owner holds 256 passages. Document t of the owner at doc index i and document t of the owner at doc index 15 - i, same qry index, have 16 + 1 passages together. `pattern`: entry [b, g] is 1 where queries b * 32 to b * 32 + 31 are scored against the documents of device g; every row has a 1.
All inputs are finite; a program needn't handle non-finite values.
Results may differ from a plain program's by a relative error of at most 0.0003.
Values may be sent and summed in bfloat16 or wider, within the bound.
No kernel may reach another device: no remote copies, remote signals or barrier semaphores. Data moves between devices by JAX's collectives and lax.ppermute only.
A program may use at most 64 MiB of HBM per device.

v0:
```python
import jax
import jax.numpy as jnp
from jax import lax
from jax.sharding import PartitionSpec as P

MAXP = 16


score_scale = 0.03125
very_negative = -1e30


def merged(array, axis, combine):
    everything = jax.tree.map(lambda part: lax.all_gather(part, axis), array)
    leading = jax.tree.map(lambda part: part[0], everything)

    def lap(k, so_far):
        return combine(so_far, jax.tree.map(lambda part: part[k], everything))

    return lax.fori_loop(1, lax.axis_size(axis), lap, leading)


def pool_first(logits, filled):
    masked = jnp.where(filled[:, None], logits, very_negative).reshape(-1, MAXP, logits.shape[1])
    highest = jnp.max(masked, axis=1)
    return highest + jnp.log(jnp.sum(jnp.exp(masked - highest[:, None, :]), axis=1))


def combine_totals(left_part, right_part):
    peak_student = jnp.maximum(left_part[0], right_part[0])
    sum_student = left_part[1] * jnp.exp(left_part[0] - peak_student) + right_part[1] * jnp.exp(
        right_part[0] - peak_student
    )
    peak_teacher = jnp.maximum(left_part[2], right_part[2])
    sum_teacher = left_part[3] * jnp.exp(left_part[2] - peak_teacher) + right_part[3] * jnp.exp(
        right_part[2] - peak_teacher
    )
    return (peak_student, sum_student, peak_teacher, sum_teacher)


def on_device(queries, passages, passage_route, pattern, teacher):
    doc_count = lax.axis_size("doc")
    query_groups = lax.axis_size("qry")
    rows_dev = queries.shape[0]
    all_queries = rows_dev * query_groups
    doc_dev = teacher.shape[1]
    table_rows = doc_dev * MAXP
    capacity = (table_rows + doc_count - 1) // doc_count
    owners = passage_route // table_rows
    target = owners // query_groups
    local_slot = passage_route - owners * table_rows
    onehot = (target[:, None] == jnp.arange(doc_count, dtype=jnp.int32)[None, :]).astype(jnp.int32)
    before = jnp.cumsum(onehot, axis=0) - onehot
    position = jnp.sum(before * onehot, axis=1)
    placing = target * capacity + position
    send_ids = (
        jnp.full((doc_count * capacity,), -1, jnp.int32)
        .at[placing]
        .set(local_slot)
        .reshape(doc_count, capacity)
    )
    got_ids = lax.all_to_all(send_ids, "doc", split_axis=0, concat_axis=0, tiled=True).reshape(-1)
    landing = jnp.where(got_ids >= 0, got_ids, table_rows)
    filled = jnp.zeros((table_rows + 1,), jnp.bool_).at[landing].set(True)[:table_rows]
    logits = (
        lax.dot_general(
            passages,
            lax.all_gather(queries, "qry", axis=0, tiled=True),
            (((1,), (1,)), ((), ())),
            preferred_element_type=jnp.float32,
        )
        * score_scale
    )
    outgoing = jnp.zeros((doc_count * capacity, all_queries), jnp.float32).at[placing].set(logits)
    outgoing = outgoing.reshape(doc_count, capacity, all_queries)
    arrived = lax.all_to_all(outgoing, "doc", split_axis=0, concat_axis=0, tiled=True).reshape(
        doc_count * capacity, all_queries
    )
    slot_scores = (
        jnp.zeros((table_rows + 1, all_queries), jnp.float32).at[landing].set(arrived)[:table_rows]
    )
    pooled = pool_first(slot_scores, filled).T
    group_id = lax.axis_index("doc") * query_groups + lax.axis_index("qry")
    column = lax.dynamic_index_in_dim(pattern, group_id, 1, keepdims=False)
    active = jnp.repeat(column, rows_dev) > 0
    doc_scores = jnp.where(active[:, None], pooled, jnp.float32(0.0))
    peak_student = jnp.max(pooled, axis=1)
    sum_student = jnp.sum(jnp.exp(pooled - peak_student[:, None]), axis=1)
    peak_teacher = jnp.max(teacher, axis=1)
    teacher_weights = jnp.exp(teacher - peak_teacher[:, None])
    sum_teacher = jnp.sum(teacher_weights, axis=1)
    local_totals = (
        jnp.where(active, peak_student, very_negative),
        jnp.where(active, sum_student, jnp.float32(0.0)),
        jnp.where(active, peak_teacher, very_negative),
        jnp.where(active, sum_teacher, jnp.float32(0.0)),
    )
    totals = merged(local_totals, ("doc", "qry"), combine_totals)
    global_weights = jnp.exp(teacher - totals[2][:, None])
    terms = jnp.where(
        active, jnp.sum(global_weights * (teacher - pooled), axis=1), jnp.float32(0.0)
    )
    weighted = lax.psum(terms, ("doc", "qry"))
    divergence_all = (
        weighted / totals[3] - totals[2] - jnp.log(totals[3]) + totals[0] + jnp.log(totals[1])
    )
    divergence = lax.dynamic_slice_in_dim(
        divergence_all, lax.axis_index("qry") * rows_dev, rows_dev
    )
    return (doc_scores, divergence)


def solution(mesh):
    in_specs = (
        P("qry", None),
        P(("doc", "qry"), None),
        P(("doc", "qry")),
        P(),
        P(None, ("doc", "qry")),
    )
    out_specs = (P(None, ("doc", "qry")), P("qry"))
    return jax.shard_map(
        on_device, mesh=mesh, in_specs=in_specs, out_specs=out_specs, check_vma=False
    )
```

profile of v0, /device:TPU:0, one launch (start us, length us, event | category | flops | bytes accessed | tf_op | source)
XLA Modules:
  0.0 223.1 jit_solution(2078619453569674549)
XLA Ops:
  0.6 0.0 copy-start
  0.6 0.8 multiply_subtract_fusion
  1.5 0.6 reduce-window.6
  2.1 0.2 slice_reduce_fusion
  2.3 0.1 bitcast_bitcast_fusion
  2.4 1.0 scatter_custom_fusion
  3.4 0.7 all_to_all.9
  4.1 8.3 %all-to-all-start = ((s32[16,1,16]{2,1,0:T(1,128)}), s32[16,1,16]{2,1,0:T(1,128)S(1)}, u32[]{:S(2)}, u32[]{:S(2)}) async-start(s32[16,1,16]{2,1,0:T(1,128)} %all_to_all.9), calls=%async_computation | async-start | bytes 16384 | tf_op jit(solution)/shard_map/all_to_all | solution.py:62
  12.4 0.0 copy-start.2
  12.5 2.4 %all_gather.19 = bf16[64,4096]{1,0:T(8,128)(2,1)S(1)} all-gather(bf16[32,4096]{1,0:T(8,128)(2,1)} %param.7), channel_id=1, replica_groups=mesh['doc'=16,'qry'=2] {'qry'}, dimensions={0}, use_global_device_ids=true | all-gather | bytes 786432 | tf_op jit(solution)/shard_map/all_gather | solution.py:68
  14.8 0.0 copy-done
  14.8 0.0 copy-start.1
  14.9 0.5 convolution_multiply_fusion
  15.4 0.0 copy-done.2
  15.4 0.2 compare_reduce_fusion
  15.6 0.1 broadcast_in_dim.73
  15.7 0.1 gt.45
  15.7 0.1 gt.44
  15.8 0.1 copy.15
  15.9 0.9 scatter_custom_fusion.2
  16.9 0.7 reshape.206
  17.6 0.0 copy-done.1
  17.6 2.0 all-to-all-done
  19.6 4.9 %all-to-all-start.1 = ((f32[16,1,1024]{2,1,0:T(1,128)}), f32[16,1,1024]{2,1,0:T(1,128)S(1)}, u32[]{:S(2)}, u32[]{:S(2)}) async-start(f32[16,1,1024]{2,1,0:T(1,128)} %reshape.206), calls=%async_computation.1 | async-start | bytes 131072 | tf_op jit(solution)/shard_map/all_to_all | solution.py:76
  24.6 0.5 broadcast.151
  25.1 0.7 reduce.8
  25.8 0.1 reshape.132
  25.9 1.5 scatter_custom_fusion.1
  27.3 4.8 %all-to-all-done.1 = f32[16,1,1024]{2,1,0:T(1,128)S(1)} async-done(((f32[16,1,1024]{2,1,0:T(1,128)}), f32[16,1,1024]{2,1,0:T(1,128)S(1)}, u32[]{:S(2)}, u32[]{:S(2)}) %all-to-all-start.1) | async-done | bytes 65568 | tf_op jit(solution)/shard_map/all_to_all | solution.py:76
  32.1 0.5 broadcast.159
  32.6 0.8 reduce.9
  33.4 0.1 reshape.207
  33.5 1.2 scatter_custom_fusion.3
  34.7 0.1 bitcast_reduce_fusion
  34.8 0.1 fusion.11
  35.0 37.1 %all-gather.3 = f32[32,1,64]{2,1,0:T(1,128)S(1)} all-gather(f32[1,1,64]{2,1,0:T(1,128)S(1)} %get-tuple-element.259), channel_id=1, replica_groups=mesh['doc'=16,'qry'=2] {'doc','qry'}, dimensions={0}, use_global_device_ids=true | all-gather | bytes 8448 | tf_op jit(solution)/shard_map/all_gather | solution.py:14
  72.1 37.2 %all-gather.2 = f32[32,1,64]{2,1,0:T(1,128)S(1)} all-gather(f32[1,1,64]{2,1,0:T(1,128)S(1)} %get-tuple-element.260), channel_id=1, replica_groups=mesh['doc'=16,'qry'=2] {'doc','qry'}, dimensions={0}, use_global_device_ids=true | all-gather | bytes 8448 | tf_op jit(solution)/shard_map/all_gather | solution.py:14
  109.2 37.0 %all-gather.1 = f32[32,1,64]{2,1,0:T(1,128)S(1)} all-gather(f32[1,1,64]{2,1,0:T(1,128)S(1)} %get-tuple-element.261), channel_id=1, replica_groups=mesh['doc'=16,'qry'=2] {'doc','qry'}, dimensions={0}, use_global_device_ids=true | all-gather | bytes 8448 | tf_op jit(solution)/shard_map/all_gather | solution.py:14
  146.3 37.2 %all-gather = f32[32,1,64]{2,1,0:T(1,128)S(1)} all-gather(f32[1,1,64]{2,1,0:T(1,128)S(1)} %get-tuple-element.262), channel_id=1, replica_groups=mesh['doc'=16,'qry'=2] {'doc','qry'}, dimensions={0}, use_global_device_ids=true | all-gather | bytes 8448 | tf_op jit(solution)/shard_map/all_gather | solution.py:14
  183.4 1.6 while.21
  185.0 0.6 fusion.21
  185.6 36.9 %psum.7 = f32[64]{0:T(128)S(1)} all-reduce(f32[64]{0:T(128)S(1)} %broadcast_select_fusion), channel_id=1, replica_groups=mesh['doc'=16,'qry'=2] {'doc','qry'}, use_global_device_ids=true, to_apply=%region_16.17 | all-reduce | flops 64 | bytes 512 | tf_op jit(solution)/shard_map/psum | solution.py:103
  222.5 0.6 dynamic_slice.48
  (50 shorter events, 1.2 us)
Async XLA Ops:
  0.6 14.2 %copy-start = (bf16[136,4096]{1,0:T(8,128)(2,1)S(1)}, bf16[136,4096]{1,0:T(8,128)(2,1)}, u32[]{:S(2)}) copy-start(bf16[136,4096]{1,0:T(8,128)(2,1)} %param.8) | copy-start | bytes 3342340
  4.1 15.5 %all-to-all-start = ((s32[16,1,16]{2,1,0:T(1,128)}), s32[16,1,16]{2,1,0:T(1,128)S(1)}, u32[]{:S(2)}, u32[]{:S(2)}) async-start(s32[16,1,16]{2,1,0:T(1,128)} %all_to_all.9), calls=%async_computation | async-start | bytes 16384 | tf_op jit(solution)/shard_map/all_to_all | solution.py:62
  12.4 2.9 %copy-start.2 = (s32[2,32]{1,0:T(2,128)S(1)}, s32[2,32]{1,0:T(2,128)}, u32[]{:S(2)}) copy-start(s32[2,32]{1,0:T(2,128)} %param.10) | copy-start | bytes 772
  14.8 2.8 %copy-start.1 = (f32[64,16]{0,1:T(8,128)S(1)}, f32[64,16]{0,1:T(8,128)}, u32[]{:S(2)}) copy-start(f32[64,16]{0,1:T(8,128)} %param.11) | copy-start | bytes 12292
  19.6 12.5 %all-to-all-start.1 = ((f32[16,1,1024]{2,1,0:T(1,128)}), f32[16,1,1024]{2,1,0:T(1,128)S(1)}, u32[]{:S(2)}, u32[]{:S(2)}) async-start(f32[16,1,1024]{2,1,0:T(1,128)} %reshape.206), calls=%async_computation.1 | async-start | bytes 131072 | tf_op jit(solution)/shard_map/all_to_all | solution.py:76
where the time goes:
time: 224 us; the launch traced here: 223 us
  blocking collectives  188 us (84%)
  starting transfers between devices  13.2 us (6%)
  local copies, waits for them, and re-layouts  8.37 us (4%)
  waiting for transfers between devices  6.75 us (3%)
  other arithmetic  5.11 us (2%)
    all_gather x4, blocking collectives, merged(): everything = jax.tree.map(lambda part: lax.all_gather(part, axis), array)  148 us
    psum x1, blocking collectives, on_device(): weighted = lax.psum(terms, ('doc', 'qry'))  36.9 us
    all_to_all x1, starting transfers between devices, on_device(): lax.all_to_all(send_ids, 'doc', split_axis=0, concat_axis=0, tiled=True)  8.31 us
    all_to_all x1, starting transfers between devices, on_device(): lax.all_to_all(outgoing, 'doc', split_axis=0, concat_axis=0, tiled=True)  4.92 us
    all_to_all x1, waiting for transfers between devices, on_device(): lax.all_to_all(outgoing, 'doc', split_axis=0, concat_axis=0, tiled=True)  4.75 us
  transfers between devices with their start and end apart: 2, of which 2 were waited for; matrix products, arithmetic and copies ran while one was open for 2% of the time, Pallas kernels for 0%

commit v1 on v0

v1 whole, which is shorter than its diff:
```python
import functools

import jax
import jax.numpy as jnp
from jax import lax
from jax.experimental import pallas as pl
from jax.experimental.pallas import tpu as pltpu
from jax.sharding import PartitionSpec as P

MAXP = 16
LANES = 128

score_scale = 0.03125
very_negative = -1e30

VMEM = pl.BlockSpec(memory_space=pltpu.VMEM)
SMEM = pl.BlockSpec(memory_space=pltpu.SMEM)
NT = (((1,), (1,)), ((), ()))


def dot_nt(a, b):
    return lax.dot_general(a, b, NT, preferred_element_type=jnp.float32)


def route_kernel(doc_count, capacity, table_rows, query_groups, route_ref, place_ref, ids_ref):
    rows = route_ref.shape[1]
    route = route_ref[...]
    owner = route // table_rows
    target = owner // query_groups
    slot = route - owner * table_rows
    down = lax.broadcasted_iota(jnp.int32, (rows, rows), 0)
    across = lax.broadcasted_iota(jnp.int32, (rows, rows), 1)

    def as_column(row):
        row = jnp.broadcast_to(row.astype(jnp.float32), (rows, rows))
        return jnp.sum(jnp.where(down == across, row, 0.0), axis=1, keepdims=True)

    target_row = target.astype(jnp.float32)
    target_column = as_column(target)
    earlier = (target_column == target_row) & (down < across)
    position = jnp.sum(jnp.where(earlier, 1.0, 0.0), axis=0, keepdims=True)
    placing = target_row * capacity + position
    outgoing = lax.broadcasted_iota(jnp.int32, (doc_count * capacity, rows), 0).astype(jnp.float32)
    place_ref[...] = jnp.where(outgoing == placing, 1.0, 0.0).astype(place_ref.dtype)
    ids_ref[...] = jnp.broadcast_to(as_column(slot) + 1.0, ids_ref.shape).astype(ids_ref.dtype)


def pack_kernel(own_first_ref, passages_ref, own_ref, *refs):
    other_refs, (place_ref, ids_ref, out_ref) = refs[:-3], refs[-3:]
    passages = passages_ref[...]
    logits = dot_nt(passages, own_ref[...])
    if other_refs:
        other = dot_nt(passages, other_refs[0][...])
        logits = jnp.where(
            own_first_ref[0] == 0,
            jnp.concatenate([logits, other], axis=1),
            jnp.concatenate([other, logits], axis=1),
        )
    logits = logits * score_scale
    high = logits.astype(jnp.bfloat16)
    low = (logits - high.astype(jnp.float32)).astype(jnp.bfloat16)
    everything = jnp.concatenate([high, low, ids_ref[...]], axis=1)
    out_ref[...] = jnp.dot(
        place_ref[...], everything, preferred_element_type=jnp.float32
    ).astype(out_ref.dtype)


def pool_kernel(rows_dev, query_groups, active_ref, arrived_ref, teacher_ref, scores_ref, out_ref):
    all_queries, doc_dev = teacher_ref.shape
    table_rows = doc_dev * MAXP
    arrived = arrived_ref[...]
    ids = arrived[:, 2 * all_queries :]
    first = jnp.where(lax.broadcasted_iota(jnp.int32, (8, LANES), 1) == 0, 1.0, 0.0)
    id_row = dot_nt(first.astype(jnp.bfloat16), ids)[:1]
    slots = lax.broadcasted_iota(jnp.int32, (table_rows, arrived.shape[0]), 0)
    wanted = (slots % doc_dev) * MAXP + slots // doc_dev + 1
    chosen = jnp.where(wanted.astype(jnp.float32) == id_row, 1.0, 0.0).astype(jnp.bfloat16)
    table = jnp.dot(chosen, arrived, preferred_element_type=jnp.float32)
    scores = table[:, :all_queries] + table[:, all_queries : 2 * all_queries]
    filled = table[:, 2 * all_queries :][:, :1] > 0.0
    masked = jnp.where(filled, scores, very_negative).reshape(MAXP, doc_dev, all_queries)
    highest = jnp.max(masked, axis=0)
    pooled = highest + jnp.log(jnp.sum(jnp.exp(masked - highest[None]), axis=0))
    lane = lax.broadcasted_iota(jnp.int32, (1, all_queries), 1)
    active = jnp.zeros((1, all_queries), jnp.bool_)
    for block in range(query_groups):
        inside = (lane >= block * rows_dev) & (lane < (block + 1) * rows_dev)
        active = active | (inside & (active_ref[block] > 0))
    scores_ref[...] = jnp.where(active, pooled, 0.0).T
    teacher = teacher_ref[...].T
    peak_student = jnp.max(pooled, axis=0, keepdims=True)
    student = peak_student + jnp.log(jnp.sum(jnp.exp(pooled - peak_student), axis=0, keepdims=True))
    peak_teacher = jnp.max(teacher, axis=0, keepdims=True)
    weights = jnp.exp(teacher - peak_teacher)
    weight_sum = jnp.sum(weights, axis=0, keepdims=True)
    mean = jnp.sum(weights * (teacher - pooled), axis=0, keepdims=True) / weight_sum
    student = jnp.where(active, student, very_negative)
    teacher_total = jnp.where(active, peak_teacher + jnp.log(weight_sum), very_negative)
    mean = jnp.where(active, mean, 0.0)
    lines = out_ref.shape[0]
    group = lax.broadcasted_iota(jnp.int32, out_ref.shape, 0) % query_groups
    out = jnp.zeros(out_ref.shape, jnp.float32)
    for block in range(query_groups):
        part = slice(block * rows_dev, (block + 1) * rows_dev)
        line = jnp.concatenate(
            [
                student[:, part],
                teacher_total[:, part],
                mean[:, part],
                jnp.zeros((1, out_ref.shape[1] - 3 * rows_dev), jnp.float32),
            ],
            axis=1,
        )
        out = jnp.where(group == block, jnp.broadcast_to(line, (lines, out_ref.shape[1])), out)
    out_ref[...] = out


def merge_kernel(rows_dev, parts_ref, out_ref):
    parts = parts_ref[...]
    student = parts[:, :rows_dev]
    teacher = parts[:, rows_dev : 2 * rows_dev]
    mean = parts[:, 2 * rows_dev : 3 * rows_dev]
    peak_student = jnp.max(student, axis=0, keepdims=True)
    student_total = peak_student + jnp.log(
        jnp.sum(jnp.exp(student - peak_student), axis=0, keepdims=True)
    )
    peak_teacher = jnp.max(teacher, axis=0, keepdims=True)
    weights = jnp.exp(teacher - peak_teacher)
    weight_sum = jnp.sum(weights, axis=0, keepdims=True)
    weighted = jnp.sum(weights * mean, axis=0, keepdims=True) / weight_sum
    out_ref[...] = weighted - (peak_teacher + jnp.log(weight_sum)) + student_total


def call(kernel, out_shape, in_specs, **cost):
    several = isinstance(out_shape, (list, tuple))
    return pl.pallas_call(
        kernel,
        out_shape=out_shape,
        in_specs=in_specs,
        out_specs=[VMEM] * len(out_shape) if several else VMEM,
        compiler_params=pltpu.CompilerParams(vmem_limit_bytes=16 * 1024 * 1024),
        cost_estimate=pl.CostEstimate(**cost) if cost else None,
    )


def on_device(queries, passages, passage_route, pattern, teacher):
    doc_count = lax.axis_size("doc")
    query_groups = lax.axis_size("qry")
    rows_dev, width = queries.shape
    rows = passages.shape[0]
    all_queries, doc_dev = teacher.shape
    table_rows = doc_dev * MAXP
    capacity = (table_rows + doc_count - 1) // doc_count
    core = lax.axis_index("qry")
    group_id = lax.axis_index("doc") * query_groups + core
    active = lax.dynamic_index_in_dim(pattern, group_id, 1, keepdims=False)

    if query_groups == 2:
        query_parts = [queries, lax.ppermute(queries, "qry", [(0, 1), (1, 0)])]
    else:
        query_parts = [lax.all_gather(queries, "qry", axis=0, tiled=True)]

    place, ids = call(
        functools.partial(route_kernel, doc_count, capacity, table_rows, query_groups),
        [
            jax.ShapeDtypeStruct((doc_count * capacity, rows), jnp.bfloat16),
            jax.ShapeDtypeStruct((rows, LANES), jnp.bfloat16),
        ],
        [VMEM],
        flops=rows * rows * 8,
        bytes_accessed=doc_count * capacity * rows * 2,
        transcendentals=0,
    )(passage_route.reshape(1, rows))
    outgoing = call(
        pack_kernel,
        jax.ShapeDtypeStruct((doc_count * capacity, 2 * all_queries + LANES), jnp.bfloat16),
        [SMEM] + [VMEM] * (len(query_parts) + 3),
    )(core.reshape(1), passages, *query_parts, place, ids)
    arrived = lax.all_to_all(outgoing, "doc", split_axis=0, concat_axis=0, tiled=True)
    line = -(-3 * rows_dev // LANES) * LANES
    devices = doc_count * query_groups
    doc_scores, partials = call(
        functools.partial(pool_kernel, rows_dev, query_groups),
        [
            jax.ShapeDtypeStruct((all_queries, doc_dev), jnp.float32),
            jax.ShapeDtypeStruct((devices, line), jnp.float32),
        ],
        [SMEM, VMEM, VMEM],
    )(active, arrived, teacher)
    everyone = lax.all_to_all(partials, ("doc", "qry"), split_axis=0, concat_axis=0, tiled=True)
    divergence = call(
        functools.partial(merge_kernel, rows_dev),
        jax.ShapeDtypeStruct((1, rows_dev), jnp.float32),
        [VMEM],
    )(everyone)
    return (doc_scores, divergence.reshape(rows_dev))


def solution(mesh):
    in_specs = (
        P("qry", None),
        P(("doc", "qry"), None),
        P(("doc", "qry")),
        P(),
        P(None, ("doc", "qry")),
    )
    out_specs = (P(None, ("doc", "qry")), P("qry"))
    return jax.shard_map(
        on_device, mesh=mesh, in_specs=in_specs, out_specs=out_specs, check_vma=False
    )
```

time: 224 us -> 34.9 us (0.16)
  blocking collectives: 188 us -> 0 us
  waiting for transfers between devices: 6.75 us -> 14.5 us
  other arithmetic: 5.11 us -> 0 us
  local copies, waits for them, and re-layouts: 8.37 us -> 3.83 us
  Pallas kernels: 0 us -> 4.22 us
    all_gather x5 -> x0, blocking collectives: 151 us -> none  [the longest x4 148 us: merged(): everything = jax.tree.map(lambda part: lax.all_gather(part, axis), array)]
    psum x1 -> x0, blocking collectives: 36.9 us -> none  [on_device(): weighted = lax.psum(terms, ('doc', 'qry'))]
    all_to_all x1, starting transfers between devices: 8.31 us -> 2.54 us  [on_device(): lax.all_to_all(partials, ('doc', 'qry'), split_axis=0, concat_axis=0, til...]
    scatter x4 -> x0, local copies, waits for them, and re-layouts: 4.59 us -> none  [the longest x1 1.49 us: on_device(): jnp.zeros((table_rows + 1,), jnp.bool_).at[landing].set(True)[:table_rows]]
    all_to_all x1, waiting for transfers between devices: 2 us -> 6.48 us  [on_device(): lax.all_to_all(partials, ('doc', 'qry'), split_axis=0, concat_axis=0, til...]
    pallas_call x0 -> x4, Pallas kernels: none -> 4.22 us  [the longest x1 1.7 us: on_device(): call(functools.partial(pool_kernel, rows_dev, query_groups), [jax.ShapeDt...]
    all_to_all x1, starting transfers between devices: 4.92 us -> 8.24 us  [on_device(): lax.all_to_all(outgoing, 'doc', split_axis=0, concat_axis=0, tiled=True)]
    unnamed x8 -> x12, local copies, waits for them, and re-layouts: 0.85 us -> 3.64 us
  transfers between devices with their start and end apart: 2 -> 3, of which waited for: 2 -> 3; matrix products, arithmetic and copies ran while one was open for 2% -> 3% of each run, Pallas kernels for 0% -> 0%
where the time goes in v1:
time: 34.9 us; the launch traced here: 34.6 us
  waiting for transfers between devices  14.5 us (42%)
  starting transfers between devices  11.3 us (32%)
  Pallas kernels  4.22 us (12%)
  local copies, waits for them, and re-layouts  3.83 us (11%)
  between operations  0.69 us (2%)
    all_to_all x1, starting transfers between devices, on_device(): lax.all_to_all(outgoing, 'doc', split_axis=0, concat_axis=0, tiled=True)  8.24 us
    all_to_all x1, waiting for transfers between devices, on_device(): lax.all_to_all(outgoing, 'doc', split_axis=0, concat_axis=0, tiled=True)  7.51 us
    all_to_all x1, waiting for transfers between devices, on_device(): lax.all_to_all(partials, ('doc', 'qry'), split_axis=0, concat_axis=0, til...  6.48 us
    unnamed x12, local copies, waits for them, and re-layouts  3.64 us
    all_to_all x1, starting transfers between devices, on_device(): lax.all_to_all(partials, ('doc', 'qry'), split_axis=0, concat_axis=0, til...  2.54 us
    pallas_call x1, Pallas kernels, on_device(): call(functools.partial(pool_kernel, rows_dev, query_groups), [jax.ShapeDt...  1.7 us
    pallas_call x1, Pallas kernels, on_device(): call(pack_kernel, jax.ShapeDtypeStruct((doc_count * capacity, 2 * all_que...  1.7 us
  transfers between devices with their start and end apart: 3, of which 3 were waited for; matrix products, arithmetic and copies ran while one was open for 3% of the time, Pallas kernels for 0%

profile of v1, /device:TPU:0, one launch (start us, length us, event | category | flops | bytes accessed | tf_op | source)
XLA Modules:
  0.0 34.6 jit_solution(3500091775036833800)
XLA Ops:
  0.6 0.0 copy-start
  0.6 0.5 %collective-permute-start = (bf16[32,4096]{1,0:T(8,128)(2,1)}, bf16[32,4096]{1,0:T(8,128)(2,1)S(1)}, u32[]{:S(2)}, u32[]{:S(2)}) collective-permute-start(bf16[32,4096]{1,0:T(8,128)(2,1)} %own_ref.1), channel_id=1, source_target_pairs={{0,1},{1,0},{2,3},{3,2},{4,5},{5,4},{6,7},{7,6},{8,9},{9,8},{10,11... | collective-permute-start | bytes 786440 | tf_op jit(solution)/shard_map/ppermute | solution.py:159
  1.2 0.0 copy-start.3
  1.2 0.7 %copy-done.3 = s32[136]{0:T(256)S(1)} copy-done((s32[136]{0:T(256)S(1)}, s32[136]{0:T(256)}, u32[]{:S(2)}) %copy-start.3) | copy-done | bytes 568
  1.8 0.0 copy-start.4
  1.8 0.1 shard_map.68
  2.0 0.5 %collective-permute-done.refs_0_ = bf16[32,4096]{1,0:T(8,128)(2,1)S(1)} collective-permute-done((bf16[32,4096]{1,0:T(8,128)(2,1)}, bf16[32,4096]{1,0:T(8,128)(2,1)S(1)}, u32[]{:S(2)}, u32[]{:S(2)}) %collective-permute-start) | collective-permute-done | bytes 262176 | tf_op jit(solution)/shard_map/ppermute | solution.py:159
  2.5 0.0 copy-start.1
  2.5 1.2 %copy-done.1 = bf16[136,4096]{1,0:T(8,128)(2,1)S(1)} copy-done((bf16[136,4096]{1,0:T(8,128)(2,1)S(1)}, bf16[136,4096]{1,0:T(8,128)(2,1)}, u32[]{:S(2)}) %copy-start.1) | copy-done | bytes 1114136
  3.8 0.0 copy-start.2
  3.8 0.9 %copy-done.2 = bf16[32,4096]{1,0:T(8,128)(2,1)S(1)} copy-done((bf16[32,4096]{1,0:T(8,128)(2,1)S(1)}, bf16[32,4096]{1,0:T(8,128)(2,1)}, u32[]{:S(2)}) %copy-start.2) | copy-done | bytes 262168
  4.7 1.7 %shard_map.69 = bf16[256,256]{1,0:T(8,128)(2,1)} custom-call(s32[1]{0:T(128)} %bitcast.own_first_ref, bf16[136,4096]{1,0:T(8,128)(2,1)S(1)} %copy-done.1, bf16[32,4096]{1,0:T(8,128)(2,1)S(1)} %copy-done.2, bf16[32,4096]{1,0:T(8,128)(2,1)S(1)} %collective-permute-done.refs_0_, bf16[256,136]{1,0:T(8,128)(2,1)S(1)} %get-tuple-element.6.refs_1_, ...), custom_call_target="tpu_custom_call" | custom-call | tf_op jit(solution)/shard_map/pallas_call | solution.py:174
  6.4 8.2 %all-to-all-start = ((bf16[16,16,256]{2,1,0:T(8,128)(2,1)}), bf16[16,16,256]{2,1,0:T(8,128)(2,1)S(1)}, u32[]{:S(2)}, u32[]{:S(2)}) async-start(bf16[16,16,256]{2,1,0:T(8,128)(2,1)} %bitcast.2), calls=%async_computation | async-start | bytes 262144 | tf_op jit(solution)/shard_map/all_to_all | solution.py:179
  14.7 0.0 copy-done.4
  14.7 0.1 copy.9.teacher_ref
  14.8 0.0 copy-done
  14.8 0.2 dynamic-slice_reduce_fusion.active_ref
  15.0 7.5 %all-to-all-done = bf16[16,16,256]{2,1,0:T(8,128)(2,1)S(1)} async-done(((bf16[16,16,256]{2,1,0:T(8,128)(2,1)}), bf16[16,16,256]{2,1,0:T(8,128)(2,1)S(1)}, u32[]{:S(2)}, u32[]{:S(2)}) %all-to-all-start) | async-done | bytes 131104 | tf_op jit(solution)/shard_map/all_to_all | solution.py:179
  22.5 1.7 %shard_map.70 = (f32[64,16]{1,0:T(8,128)S(1)}, f32[32,128]{1,0:T(8,128)}) custom-call(s32[2]{0:T(128)S(1)} %dynamic-slice_reduce_fusion.active_ref, bf16[256,256]{1,0:T(8,128)(2,1)S(1)} %bitcast.9, f32[64,16]{1,0:T(8,128)S(1)} %copy.9.teacher_ref), custom_call_target="tpu_custom_call" | custom-call | tf_op jit(solution)/shard_map/pallas_call | solution.py:182
  24.2 2.5 %all-to-all-start.1 = ((f32[32,1,128]{2,1,0:T(1,128)}), f32[32,1,128]{2,1,0:T(1,128)S(1)}, u32[]{:S(2)}, u32[]{:S(2)}) async-start(f32[32,1,128]{2,1,0:T(1,128)} %bitcast.5), calls=%async_computation.1 | async-start | bytes 32768 | tf_op jit(solution)/shard_map/all_to_all | solution.py:190
  26.7 0.7 %copy.11 = f32[64,16]{0,1:T(8,128)} copy(f32[64,16]{1,0:T(8,128)S(1)} %get-tuple-element.12) | data formatting | bytes 8192
  27.4 6.5 %all-to-all-done.1 = f32[32,1,128]{2,1,0:T(1,128)S(1)} async-done(((f32[32,1,128]{2,1,0:T(1,128)}), f32[32,1,128]{2,1,0:T(1,128)S(1)}, u32[]{:S(2)}, u32[]{:S(2)}) %all-to-all-start.1) | async-done | bytes 16416 | tf_op jit(solution)/shard_map/all_to_all | solution.py:190
  33.9 0.7 %shard_map.71 = f32[1,32]{1,0:T(1,128)} custom-call(f32[32,128]{1,0:T(8,128)S(1)} %bitcast.10), custom_call_target="tpu_custom_call" | custom-call | tf_op jit(solution)/shard_map/pallas_call | solution.py:191
Async XLA Ops:
  0.6 14.2 %copy-start = (s32[2,32]{1,0:T(2,128)S(1)}, s32[2,32]{1,0:T(2,128)}, u32[]{:S(2)}) copy-start(s32[2,32]{1,0:T(2,128)} %param.8) | copy-start | bytes 772
  0.6 1.9 %collective-permute-start = (bf16[32,4096]{1,0:T(8,128)(2,1)}, bf16[32,4096]{1,0:T(8,128)(2,1)S(1)}, u32[]{:S(2)}, u32[]{:S(2)}) collective-permute-start(bf16[32,4096]{1,0:T(8,128)(2,1)} %own_ref.1), channel_id=1, source_target_pairs={{0,1},{1,0},{2,3},{3,2},{4,5},{5,4},{6,7},{7,6},{8,9},{9,8},{10,11... | collective-permute-start | bytes 786440 | tf_op jit(solution)/shard_map/ppermute | solution.py:159
  1.2 0.7 %copy-start.3 = (s32[136]{0:T(256)S(1)}, s32[136]{0:T(256)}, u32[]{:S(2)}) copy-start(s32[136]{0:T(256)} %param.7) | copy-start | bytes 1636
  1.8 12.8 %copy-start.4 = (f32[64,16]{0,1:T(8,128)S(1)}, f32[64,16]{0,1:T(8,128)}, u32[]{:S(2)}) copy-start(f32[64,16]{0,1:T(8,128)} %param.9) | copy-start | bytes 12292
  2.5 1.2 %copy-start.1 = (bf16[136,4096]{1,0:T(8,128)(2,1)S(1)}, bf16[136,4096]{1,0:T(8,128)(2,1)}, u32[]{:S(2)}) copy-start(bf16[136,4096]{1,0:T(8,128)(2,1)} %passages_ref.1) | copy-start | bytes 3342340
  3.8 0.9 %copy-start.2 = (bf16[32,4096]{1,0:T(8,128)(2,1)S(1)}, bf16[32,4096]{1,0:T(8,128)(2,1)}, u32[]{:S(2)}) copy-start(bf16[32,4096]{1,0:T(8,128)(2,1)} %own_ref.1) | copy-start | bytes 786436
  6.4 16.0 %all-to-all-start = ((bf16[16,16,256]{2,1,0:T(8,128)(2,1)}), bf16[16,16,256]{2,1,0:T(8,128)(2,1)S(1)}, u32[]{:S(2)}, u32[]{:S(2)}) async-start(bf16[16,16,256]{2,1,0:T(8,128)(2,1)} %bitcast.2), calls=%async_computation | async-start | bytes 262144 | tf_op jit(solution)/shard_map/all_to_all | solution.py:179
  24.2 9.7 %all-to-all-start.1 = ((f32[32,1,128]{2,1,0:T(1,128)}), f32[32,1,128]{2,1,0:T(1,128)S(1)}, u32[]{:S(2)}, u32[]{:S(2)}) async-start(f32[32,1,128]{2,1,0:T(1,128)} %bitcast.5), calls=%async_computation.1 | async-start | bytes 32768 | tf_op jit(solution)/shard_map/all_to_all | solution.py:190

commit v2 on v1

v2 whole, which is shorter than its diff:
```python
import functools

import jax
import jax.numpy as jnp
from jax import lax
from jax.experimental import pallas as pl
from jax.experimental.pallas import tpu as pltpu
from jax.sharding import PartitionSpec as P

MAXP = 16
LANES = 128
SUBLANES = 8
CHUNKS = 4

score_scale = 0.03125
very_negative = -1e30

VMEM = pl.BlockSpec(memory_space=pltpu.VMEM)
HBM = pl.BlockSpec(memory_space=pltpu.HBM)
NT = (((1,), (1,)), ((), ()))


def dot_nt(a, b):
    return lax.dot_general(a, b, NT, preferred_element_type=jnp.float32)


def halves(logits):
    high = logits.astype(jnp.bfloat16)
    return high, (logits - high.astype(jnp.float32)).astype(jnp.bfloat16)


def before_kernel(
    sizes, passages_hbm, own_hbm, route_hbm, pattern_hbm, teacher_hbm,
    passages_ref, logits_ref, place_ref, ids_ref, weights_ref, notes_ref,
    own_ref, route_ref, pattern_ref, teacher_ref, passages_sem, small_sem,
):
    doc_count, query_groups, capacity, table_rows, rows_dev = sizes
    rows, width = passages_ref.shape
    step = width // CHUNKS
    copies = []
    for chunk in range(CHUNKS):
        part = pl.ds(chunk * step, step)
        copies.append(
            pltpu.make_async_copy(
                passages_hbm.at[:, part], passages_ref.at[:, part], passages_sem.at[chunk]
            )
        )
    small = [
        pltpu.make_async_copy(source, target, small_sem.at[k])
        for k, (source, target) in enumerate(
            [
                (route_hbm, route_ref),
                (pattern_hbm, pattern_ref),
                (teacher_hbm, teacher_ref),
                (own_hbm, own_ref),
            ]
        )
    ]
    for copy in small + copies:
        copy.start()
    core = lax.axis_index("qry")
    group_id = lax.axis_index("doc") * query_groups + core

    small[0].wait()
    route = route_ref[...]
    owner = route // table_rows
    target = (owner // query_groups).astype(jnp.float32)
    slot = (route - owner * table_rows).astype(jnp.float32)
    down = lax.broadcasted_iota(jnp.int32, (rows, rows), 0)
    across = lax.broadcasted_iota(jnp.int32, (rows, rows), 1)

    def as_column(row):
        row = jnp.broadcast_to(row, (rows, rows))
        return jnp.sum(jnp.where(down == across, row, 0.0), axis=1, keepdims=True)

    earlier = (as_column(target) == target) & (down < across)
    position = jnp.sum(jnp.where(earlier, 1.0, 0.0), axis=0, keepdims=True)
    placing = target * capacity + position
    outgoing = lax.broadcasted_iota(jnp.int32, (doc_count * capacity, rows), 0).astype(jnp.float32)
    place_ref[...] = jnp.where(outgoing == placing, 1.0, 0.0).astype(place_ref.dtype)
    ids_ref[...] = jnp.broadcast_to(as_column(slot) + 1.0, ids_ref.shape).astype(ids_ref.dtype)

    small[1].wait()
    all_queries = rows_dev * query_groups
    lane = lax.broadcasted_iota(jnp.int32, (1, all_queries), 1)
    mine = lax.broadcasted_iota(jnp.int32, pattern_ref.shape, 1) == group_id
    flags = jnp.sum(jnp.where(mine, pattern_ref[...], 0), axis=1, keepdims=True)
    active = jnp.zeros((1, all_queries), jnp.float32)
    for block in range(query_groups):
        inside = (lane >= block * rows_dev) & (lane < (block + 1) * rows_dev)
        flag = jnp.broadcast_to(flags[block : block + 1], (1, all_queries))
        active = jnp.where(inside & (flag > 0), 1.0, active)
    small[2].wait()
    teacher = teacher_ref[...]
    peak = jnp.max(teacher, axis=0, keepdims=True)
    weights = jnp.exp(teacher - peak)
    weight_sum = jnp.sum(weights, axis=0, keepdims=True)
    weights = weights / weight_sum
    weights_ref[...] = weights
    notes_ref[0:1, :] = jnp.where(active > 0.0, peak + jnp.log(weight_sum), very_negative)
    notes_ref[1:2, :] = jnp.sum(weights * teacher, axis=0, keepdims=True)
    notes_ref[2:3, :] = active
    notes_ref[3:4, :] = jnp.full((1, all_queries), core, jnp.int32).astype(jnp.float32)
    notes_ref[4:, :] = jnp.zeros((notes_ref.shape[0] - 4, all_queries), jnp.float32)

    small[3].wait()
    logits = jnp.zeros((rows, rows_dev), jnp.float32)
    for chunk in range(CHUNKS):
        part = pl.ds(chunk * step, step)
        copies[chunk].wait()
        logits += dot_nt(passages_ref[:, part], own_ref[:, part])
    logits_ref[...] = logits * score_scale


def pack_kernel(passages_ref, logits_ref, place_ref, ids_ref, *refs):
    other_refs, out_ref = refs[:-1], refs[-1]
    passages = passages_ref[...]
    parts = [halves(logits_ref[...])]
    parts += [halves(dot_nt(passages, other[...]) * score_scale) for other in other_refs]
    columns = [high for high, low in parts] + [low for high, low in parts] + [ids_ref[...]]
    out_ref[...] = jnp.dot(
        place_ref[...], jnp.concatenate(columns, axis=1), preferred_element_type=jnp.float32
    ).astype(out_ref.dtype)


def pool_kernel(rows_dev, query_groups, arrived_ref, weights_ref, notes_ref, scores_ref, out_ref):
    doc_dev, all_queries = weights_ref.shape
    table_rows = doc_dev * MAXP
    slots = arrived_ref.shape[0]
    first = jnp.where(lax.broadcasted_iota(jnp.int32, (SUBLANES, LANES), 1) == 0, 1.0, 0.0)
    id_row = dot_nt(first.astype(jnp.bfloat16), arrived_ref[:, 2 * all_queries :])[:1]
    shape = (MAXP, doc_dev, slots)
    wanted = lax.broadcasted_iota(jnp.int32, shape, 0) + lax.broadcasted_iota(jnp.int32, shape, 1) * MAXP
    wanted = wanted.reshape(table_rows, slots).astype(jnp.float32) + 1.0
    chosen = jnp.where(wanted == id_row, 1.0, 0.0).astype(jnp.bfloat16)
    table = jnp.dot(chosen, arrived_ref[:, : 2 * all_queries], preferred_element_type=jnp.float32)
    scores = table[:, :all_queries] + table[:, all_queries:]
    document = lax.broadcasted_iota(jnp.int32, (doc_dev, slots), 0).astype(jnp.float32)
    held = jnp.floor((id_row - 1.0) * (1.0 / MAXP)) == document
    count = jnp.sum(jnp.where(held, 1.0, 0.0), axis=1, keepdims=True)
    count = jnp.broadcast_to(count, (doc_dev, all_queries))
    scores = scores.reshape(MAXP, doc_dev, all_queries)
    places = [jnp.where(count > place, scores[place], very_negative) for place in range(MAXP)]
    highest = functools.reduce(jnp.maximum, places)
    total = functools.reduce(jnp.add, [jnp.exp(place - highest) for place in places])
    pooled = highest + jnp.log(total)
    if query_groups > 1:
        core = notes_ref[3:4, :]
        ordered = pooled
        for mine in range(1, query_groups):
            cut = all_queries - mine * rows_dev
            turned = jnp.concatenate([pooled[:, cut:], pooled[:, :cut]], axis=1)
            ordered = jnp.where(core == float(mine), turned, ordered)
        pooled = ordered
    active = notes_ref[2:3, :] > 0.0
    scores_ref[...] = jnp.where(active, pooled, 0.0)
    peak = jnp.max(pooled, axis=0, keepdims=True)
    student = peak + jnp.log(jnp.sum(jnp.exp(pooled - peak), axis=0, keepdims=True))
    student = jnp.where(active, student, very_negative)
    mean = notes_ref[1:2, :] - jnp.sum(weights_ref[...] * pooled, axis=0, keepdims=True)
    teacher = notes_ref[0:1, :]
    group = lax.broadcasted_iota(jnp.int32, out_ref.shape, 0) % query_groups
    out = jnp.zeros(out_ref.shape, jnp.float32)
    for block in range(query_groups):
        part = slice(block * rows_dev, (block + 1) * rows_dev)
        line = jnp.concatenate(
            [
                student[:, part],
                teacher[:, part],
                mean[:, part],
                jnp.zeros((1, out_ref.shape[1] - 3 * rows_dev), jnp.float32),
            ],
            axis=1,
        )
        out = jnp.where(group == block, jnp.broadcast_to(line, out_ref.shape), out)
    out_ref[...] = out


def merge_kernel(rows_dev, parts_ref, scores_in_ref, out_ref, scores_ref):
    scores_ref[...] = scores_in_ref[...]
    parts = parts_ref[...]
    student = parts[:, :rows_dev]
    teacher = parts[:, rows_dev : 2 * rows_dev]
    mean = parts[:, 2 * rows_dev : 3 * rows_dev]
    peak_student = jnp.max(student, axis=0, keepdims=True)
    student_total = peak_student + jnp.log(
        jnp.sum(jnp.exp(student - peak_student), axis=0, keepdims=True)
    )
    peak_teacher = jnp.max(teacher, axis=0, keepdims=True)
    weights = jnp.exp(teacher - peak_teacher)
    weight_sum = jnp.sum(weights, axis=0, keepdims=True)
    weighted = jnp.sum(weights * mean, axis=0, keepdims=True) / weight_sum
    out_ref[...] = weighted - (peak_teacher + jnp.log(weight_sum)) + student_total


def call(kernel, out_shape, in_specs, scratch=(), **cost):
    several = isinstance(out_shape, (list, tuple))
    return pl.pallas_call(
        kernel,
        out_shape=out_shape,
        in_specs=in_specs,
        out_specs=[VMEM] * len(out_shape) if several else VMEM,
        scratch_shapes=scratch,
        compiler_params=pltpu.CompilerParams(vmem_limit_bytes=16 * 1024 * 1024),
        cost_estimate=pl.CostEstimate(**cost) if cost else None,
    )


def on_device(queries, passages, passage_route, pattern, teacher):
    doc_count = lax.axis_size("doc")
    query_groups = lax.axis_size("qry")
    devices = doc_count * query_groups
    rows_dev, width = queries.shape
    rows = passages.shape[0]
    all_queries, doc_dev = teacher.shape
    table_rows = doc_dev * MAXP
    capacity = (table_rows + doc_count - 1) // doc_count
    f32, bf16 = jnp.float32, jnp.bfloat16
    shaped = jax.ShapeDtypeStruct

    others = [
        lax.ppermute(queries, "qry", [((i + k) % query_groups, i) for i in range(query_groups)])
        for k in range(1, query_groups)
    ]
    held, logits, place, ids, weights, notes = call(
        functools.partial(
            before_kernel, (doc_count, query_groups, capacity, table_rows, rows_dev)
        ),
        [
            shaped((rows, width), bf16),
            shaped((rows, rows_dev), f32),
            shaped((doc_count * capacity, rows), bf16),
            shaped((rows, LANES), bf16),
            shaped((doc_dev, all_queries), f32),
            shaped((SUBLANES, all_queries), f32),
        ],
        [HBM] * 5,
        [
            pltpu.VMEM((rows_dev, width), bf16),
            pltpu.VMEM((1, rows), jnp.int32),
            pltpu.VMEM(pattern.shape, jnp.int32),
            pltpu.VMEM((doc_dev, all_queries), f32),
            pltpu.SemaphoreType.DMA((CHUNKS,)),
            pltpu.SemaphoreType.DMA((4,)),
        ],
        flops=2 * rows * rows_dev * width,
        bytes_accessed=2 * (rows + rows_dev) * width,
        transcendentals=0,
    )(
        *[
            pltpu.with_memory_space_constraint(array, pltpu.HBM)
            for array in (passages, queries, passage_route.reshape(1, rows), pattern, teacher.T)
        ]
    )
    outgoing = call(
        pack_kernel,
        shaped((doc_count * capacity, 2 * all_queries + LANES), bf16),
        [VMEM] * (4 + len(others)),
    )(held, logits, place, ids, *others)
    arrived = lax.all_to_all(outgoing, "doc", split_axis=0, concat_axis=0, tiled=True)
    line = -(-3 * rows_dev // LANES) * LANES
    doc_scores, partials = call(
        functools.partial(pool_kernel, rows_dev, query_groups),
        [shaped((doc_dev, all_queries), f32), shaped((devices, line), f32)],
        [VMEM, VMEM, VMEM],
    )(arrived, weights, notes)
    everyone = lax.all_to_all(partials, ("doc", "qry"), split_axis=0, concat_axis=0, tiled=True)
    divergence, doc_scores = call(
        functools.partial(merge_kernel, rows_dev),
        [shaped((1, rows_dev), f32), shaped((doc_dev, all_queries), f32)],
        [VMEM, VMEM],
    )(everyone, doc_scores)
    return (doc_scores.T, divergence.reshape(rows_dev))


def solution(mesh):
    in_specs = (
        P("qry", None),
        P(("doc", "qry"), None),
        P(("doc", "qry")),
        P(),
        P(None, ("doc", "qry")),
    )
    out_specs = (P(None, ("doc", "qry")), P("qry"))
    return jax.shard_map(
        on_device, mesh=mesh, in_specs=in_specs, out_specs=out_specs, check_vma=False
    )
```

time: 34.9 us -> 30.5 us (0.87)
  blocking collectives: 0 us -> 24.9 us
  waiting for transfers between devices: 14.5 us -> 0.01 us
  starting transfers between devices: 11.3 us -> 0.52 us
  local copies, waits for them, and re-layouts: 3.83 us -> 0 us
    all_to_all x0 -> x2, blocking collectives: none -> 24.9 us  [the longest x1 15.8 us: on_device(): lax.all_to_all(outgoing, 'doc', split_axis=0, concat_axis=0, tiled=True)]
    all_to_all x2 -> x0, waiting for transfers between devices: 14 us -> none  [the longest x1 7.51 us: on_device(): lax.all_to_all(outgoing, 'doc', split_axis=0, concat_axis=0, tiled=True)]
    all_to_all x2 -> x0, starting transfers between devices: 10.8 us -> none  [the longest x1 8.24 us: on_device(): lax.all_to_all(outgoing, 'doc', split_axis=0, concat_axis=0, tiled=True)]
    unnamed x12 -> x0, local copies, waits for them, and re-layouts: 3.64 us -> none
    ppermute x1, waiting for transfers between devices: 0.53 us -> 0.01 us  [on_device(): lax.ppermute(queries, 'qry', [((i + k) % query_groups, i) for i in range(...]
  transfers between devices with their start and end apart: 3 -> 1, of which waited for: 3 -> 0; matrix products, arithmetic and copies ran while one was open for 3% -> 0% of each run, Pallas kernels for 0% -> 7%
where the time goes in v2:
time: 30.5 us; the launch traced here: 30.3 us
  blocking collectives  24.9 us (82%)
  Pallas kernels  4.21 us (14%)
  between operations  0.66 us (2%)
  starting transfers between devices  0.52 us (2%)
    all_to_all x1, blocking collectives, on_device(): lax.all_to_all(outgoing, 'doc', split_axis=0, concat_axis=0, tiled=True)  15.8 us
    all_to_all x1, blocking collectives, on_device(): lax.all_to_all(partials, ('doc', 'qry'), split_axis=0, concat_axis=0, til...  9.11 us
    pallas_call x1, Pallas kernels, on_device(): call(functools.partial(before_kernel, (doc_count, query_groups, capacity,...  2.2 us
    pallas_call x1, Pallas kernels, on_device(): call(pack_kernel, shaped((doc_count * capacity, 2 * all_queries + LANES),...  0.73 us
    pallas_call x1, Pallas kernels, on_device(): call(functools.partial(merge_kernel, rows_dev), [shaped((1, rows_dev), f3...  0.69 us
  transfers between devices with their start and end apart: 1, of which 0 were waited for; matrix products, arithmetic and copies ran while one was open for 0% of the time, Pallas kernels for 7%

profile of v2, /device:TPU:0, one launch (start us, length us, event | category | flops | bytes accessed | tf_op | source)
XLA Modules:
  0.0 30.3 jit_solution(16542094359156350227)
XLA Ops:
  0.6 0.5 %collective-permute-start = (bf16[32,4096]{1,0:T(8,128)(2,1)}, bf16[32,4096]{1,0:T(8,128)(2,1)S(1)}, u32[]{:S(2)}, u32[]{:S(2)}) collective-permute-start(bf16[32,4096]{1,0:T(8,128)(2,1)} %own_hbm.1), channel_id=1, source_target_pairs={{1,0},{0,1},{3,2},{2,3},{5,4},{4,5},{7,6},{6,7},{9,8},{8,9},{11,10... | collective-permute-start | bytes 786440 | tf_op jit(solution)/shard_map/ppermute | solution.py:222
  1.1 2.2 %shard_map.68 = (bf16[136,4096]{1,0:T(8,128)(2,1)S(1)}, f32[136,32]{1,0:T(8,128)S(1)}, bf16[256,136]{1,0:T(8,128)(2,1)S(1)}, bf16[136,128]{1,0:T(8,128)(2,1)S(1)...) custom-call(bf16[136,4096]{1,0:T(8,128)(2,1)} %passages_hbm.1, bf16[32,4096]{1,0:T(8,128)(2,1)} %own_hbm.1, ...), custom_call_target="tpu_custom_call" | custom-call | flops 35651584 | bytes 1376256 | tf_op jit(solution)/shard_map/pallas_call | solution.py:225
  3.4 0.0 collective-permute-done.refs_0_
  3.4 0.7 %shard_map.69 = bf16[256,256]{1,0:T(8,128)(2,1)S(1)} custom-call(bf16[136,4096]{1,0:T(8,128)(2,1)S(1)} %get-tuple-element.12.passages_ref, f32[136,32]{1,0:T(8,128)S(1)} %get-tuple-element.13.logits_ref, bf16[256,136]{1,0:T(8,128)(2,1)S(1)} %get-tuple-element.14.place_ref, bf16[136,128]{1,0:T(8,128)(2,1)S(1)} %get-tuple-element.15.ids_ref, ...), custom_call_target="tpu_custom_call" | custom-call | tf_op jit(solution)/shard_map/pallas_call | solution.py:255
  4.1 15.8 %all_to_all.22 = bf16[16,16,256]{2,1,0:T(8,128)(2,1)S(1)} all-to-all(bf16[16,16,256]{2,1,0:T(8,128)(2,1)S(1)} %bitcast.11), channel_id=1, replica_groups=mesh['doc'=16,'qry'=2] {'doc'}, dimensions={0} | all-to-all | bytes 262144 | tf_op jit(solution)/shard_map/all_to_all | solution.py:260
  19.9 0.6 %shard_map.70 = (f32[16,64]{1,0:T(8,128)S(1)}, f32[32,128]{1,0:T(8,128)S(1)}) custom-call(bf16[256,256]{1,0:T(8,128)(2,1)S(1)} %bitcast.10, f32[16,64]{1,0:T(8,128)S(1)} %get-tuple-element.16.weights_ref, f32[8,64]{1,0:T(8,128)S(1)} %get-tuple-element.17.notes_ref), custom_call_target="tpu_custom_call" | custom-call | tf_op jit(solution)/shard_map/pallas_call | solution.py:262
  20.5 9.1 %all_to_all.23 = f32[32,1,128]{2,1,0:T(1,128)S(1)} all-to-all(f32[32,1,128]{2,1,0:T(1,128)S(1)} %bitcast.13), channel_id=1, replica_groups=mesh['doc'=16,'qry'=2] {'doc','qry'}, dimensions={0} | all-to-all | bytes 32768 | tf_op jit(solution)/shard_map/all_to_all | solution.py:267
  29.6 0.7 %shard_map.71 = (f32[1,32]{1,0:T(1,128)}, f32[16,64]{1,0:T(8,128)}) custom-call(f32[32,128]{1,0:T(8,128)S(1)} %bitcast.12, f32[16,64]{1,0:T(8,128)S(1)} %get-tuple-element.19.scores_in_ref), custom_call_target="tpu_custom_call" | custom-call | tf_op jit(solution)/shard_map/pallas_call | solution.py:268
Async XLA Ops:
  0.6 2.7 %collective-permute-start = (bf16[32,4096]{1,0:T(8,128)(2,1)}, bf16[32,4096]{1,0:T(8,128)(2,1)S(1)}, u32[]{:S(2)}, u32[]{:S(2)}) collective-permute-start(bf16[32,4096]{1,0:T(8,128)(2,1)} %own_hbm.1), channel_id=1, source_target_pairs={{1,0},{0,1},{3,2},{2,3},{5,4},{4,5},{7,6},{6,7},{9,8},{8,9},{11,10... | collective-permute-start | bytes 786440 | tf_op jit(solution)/shard_map/ppermute | solution.py:222

commit v3 on v2

--- a/solution.py
+++ b/solution.py
@@ -10,7 +10,6 @@
 MAXP = 16
 LANES = 128
 SUBLANES = 8
-CHUNKS = 4
 
 score_scale = 0.03125
 very_negative = -1e30
@@ -24,39 +23,27 @@
     return lax.dot_general(a, b, NT, preferred_element_type=jnp.float32)
 
 
-def halves(logits):
-    high = logits.astype(jnp.bfloat16)
-    return high, (logits - high.astype(jnp.float32)).astype(jnp.bfloat16)
-
-
 def before_kernel(
     sizes, passages_hbm, own_hbm, route_hbm, pattern_hbm, teacher_hbm,
-    passages_ref, logits_ref, place_ref, ids_ref, weights_ref, notes_ref,
-    own_ref, route_ref, pattern_ref, teacher_ref, passages_sem, small_sem,
+    passages_ref, own_ref, place_ref, ids_ref, weights_ref, notes_ref,
+    route_ref, pattern_ref, teacher_ref, passages_sem, small_sem,
 ):
     doc_count, query_groups, capacity, table_rows, rows_dev = sizes
-    rows, width = passages_ref.shape
-    step = width // CHUNKS
-    copies = []
-    for chunk in range(CHUNKS):
-        part = pl.ds(chunk * step, step)
-        copies.append(
-            pltpu.make_async_copy(
-                passages_hbm.at[:, part], passages_ref.at[:, part], passages_sem.at[chunk]
-            )
-        )
+    rows = passages_ref.shape[0]
+    pairs = [
+        (route_hbm, route_ref),
+        (pattern_hbm, pattern_ref),
+        (teacher_hbm, teacher_ref),
+        (own_hbm, own_ref),
+    ]
     small = [
         pltpu.make_async_copy(source, target, small_sem.at[k])
-        for k, (source, target) in enumerate(
-            [
-                (route_hbm, route_ref),
-                (pattern_hbm, pattern_ref),
-                (teacher_hbm, teacher_ref),
-                (own_hbm, own_ref),
-            ]
-        )
+        for k, (source, target) in enumerate(pairs)
     ]
-    for copy in small + copies:
+    large = pltpu.make_async_copy(passages_hbm, passages_ref, passages_sem)
+    small[0].start()
+    large.start()
+    for copy in small[1:]:
         copy.start()
     core = lax.axis_index("qry")
     group_id = lax.axis_index("doc") * query_groups + core
@@ -81,6 +68,7 @@
     ids_ref[...] = jnp.broadcast_to(as_column(slot) + 1.0, ids_ref.shape).astype(ids_ref.dtype)
 
     small[1].wait()
+    small[2].wait()
     all_queries = rows_dev * query_groups
     lane = lax.broadcasted_iota(jnp.int32, (1, all_queries), 1)
     mine = lax.broadcasted_iota(jnp.int32, pattern_ref.shape, 1) == group_id
@@ -90,7 +78,6 @@
         inside = (lane >= block * rows_dev) & (lane < (block + 1) * rows_dev)
         flag = jnp.broadcast_to(flags[block : block + 1], (1, all_queries))
         active = jnp.where(inside & (flag > 0), 1.0, active)
-    small[2].wait()
     teacher = teacher_ref[...]
     peak = jnp.max(teacher, axis=0, keepdims=True)
     weights = jnp.exp(teacher - peak)
@@ -102,24 +89,19 @@
     notes_ref[2:3, :] = active
     notes_ref[3:4, :] = jnp.full((1, all_queries), core, jnp.int32).astype(jnp.float32)
     notes_ref[4:, :] = jnp.zeros((notes_ref.shape[0] - 4, all_queries), jnp.float32)
-
     small[3].wait()
-    logits = jnp.zeros((rows, rows_dev), jnp.float32)
-    for chunk in range(CHUNKS):
-        part = pl.ds(chunk * step, step)
-        copies[chunk].wait()
-        logits += dot_nt(passages_ref[:, part], own_ref[:, part])
-    logits_ref[...] = logits * score_scale
-
-
-def pack_kernel(passages_ref, logits_ref, place_ref, ids_ref, *refs):
-    other_refs, out_ref = refs[:-1], refs[-1]
-    passages = passages_ref[...]
-    parts = [halves(logits_ref[...])]
-    parts += [halves(dot_nt(passages, other[...]) * score_scale) for other in other_refs]
-    columns = [high for high, low in parts] + [low for high, low in parts] + [ids_ref[...]]
+    large.wait()
+
+
+def pack_kernel(passages_ref, place_ref, ids_ref, *refs):
+    query_refs, out_ref = refs[:-1], refs[-1]
+    queries = jnp.concatenate([part[...] for part in query_refs], axis=0)
+    logits = dot_nt(passages_ref[...], queries) * score_scale
+    high = logits.astype(jnp.bfloat16)
+    low = (logits - high.astype(jnp.float32)).astype(jnp.bfloat16)
+    columns = jnp.concatenate([high, low, ids_ref[...]], axis=1)
     out_ref[...] = jnp.dot(
-        place_ref[...], jnp.concatenate(columns, axis=1), preferred_element_type=jnp.float32
+        place_ref[...], columns, preferred_element_type=jnp.float32
     ).astype(out_ref.dtype)
 
 
@@ -222,13 +204,13 @@
         lax.ppermute(queries, "qry", [((i + k) % query_groups, i) for i in range(query_groups)])
         for k in range(1, query_groups)
     ]
-    held, logits, place, ids, weights, notes = call(
+    held, own, place, ids, weights, notes = call(
         functools.partial(
             before_kernel, (doc_count, query_groups, capacity, table_rows, rows_dev)
         ),
         [
             shaped((rows, width), bf16),
-            shaped((rows, rows_dev), f32),
+            shaped((rows_dev, width), bf16),
             shaped((doc_count * capacity, rows), bf16),
             shaped((rows, LANES), bf16),
             shaped((doc_dev, all_queries), f32),
@@ -236,14 +218,13 @@
         ],
         [HBM] * 5,
         [
-            pltpu.VMEM((rows_dev, width), bf16),
             pltpu.VMEM((1, rows), jnp.int32),
             pltpu.VMEM(pattern.shape, jnp.int32),
             pltpu.VMEM((doc_dev, all_queries), f32),
-            pltpu.SemaphoreType.DMA((CHUNKS,)),
+            pltpu.SemaphoreType.DMA(()),
             pltpu.SemaphoreType.DMA((4,)),
         ],
-        flops=2 * rows * rows_dev * width,
+        flops=doc_count * capacity * rows,
         bytes_accessed=2 * (rows + rows_dev) * width,
         transcendentals=0,
     )(
@@ -256,7 +237,7 @@
         pack_kernel,
         shaped((doc_count * capacity, 2 * all_queries + LANES), bf16),
         [VMEM] * (4 + len(others)),
-    )(held, logits, place, ids, *others)
+    )(held, place, ids, own, *others)
     arrived = lax.all_to_all(outgoing, "doc", split_axis=0, concat_axis=0, tiled=True)
     line = -(-3 * rows_dev // LANES) * LANES
     doc_scores, partials = call(

time: 30.5 us -> 29.7 us (0.974)
  Pallas kernels: 4.21 us -> 3.4 us
    pallas_call x1, Pallas kernels: 2.2 us -> 1.38 us  [on_device(): call(functools.partial(before_kernel, (doc_count, query_groups, capacity,...]
  transfers between devices with their start and end apart: 1 -> 1, of which waited for: 0 -> 0; matrix products, arithmetic and copies ran while one was open for 0% -> 0% of each run, Pallas kernels for 7% -> 5%
where the time goes in v3:
time: 29.7 us; the launch traced here: 29.5 us
  blocking collectives  24.9 us (84%)
  Pallas kernels  3.4 us (11%)
  between operations  0.66 us (2%)
  starting transfers between devices  0.52 us (2%)
    all_to_all x1, blocking collectives, on_device(): lax.all_to_all(outgoing, 'doc', split_axis=0, concat_axis=0, tiled=True)  15.8 us
    all_to_all x1, blocking collectives, on_device(): lax.all_to_all(partials, ('doc', 'qry'), split_axis=0, concat_axis=0, til...  9.07 us
    pallas_call x1, Pallas kernels, on_device(): call(functools.partial(before_kernel, (doc_count, query_groups, capacity,...  1.38 us
    pallas_call x1, Pallas kernels, on_device(): call(pack_kernel, shaped((doc_count * capacity, 2 * all_queries + LANES),...  0.74 us
    pallas_call x1, Pallas kernels, on_device(): call(functools.partial(merge_kernel, rows_dev), [shaped((1, rows_dev), f3...  0.69 us
  transfers between devices with their start and end apart: 1, of which 0 were waited for; matrix products, arithmetic and copies ran while one was open for 0% of the time, Pallas kernels for 5%

profile of v3, /device:TPU:0, one launch (start us, length us, event | category | flops | bytes accessed | tf_op | source)
XLA Modules:
  0.0 29.5 jit_solution(2849522550311947836)
XLA Ops:
  0.6 0.5 %collective-permute-start = (bf16[32,4096]{1,0:T(8,128)(2,1)}, bf16[32,4096]{1,0:T(8,128)(2,1)S(1)}, u32[]{:S(2)}, u32[]{:S(2)}) collective-permute-start(bf16[32,4096]{1,0:T(8,128)(2,1)} %own_hbm.1), channel_id=1, source_target_pairs={{1,0},{0,1},{3,2},{2,3},{5,4},{4,5},{7,6},{6,7},{9,8},{8,9},{11,10... | collective-permute-start | bytes 786440 | tf_op jit(solution)/shard_map/ppermute | solution.py:204
  1.1 1.4 %shard_map.68 = (bf16[136,4096]{1,0:T(8,128)(2,1)S(1)}, bf16[32,4096]{1,0:T(8,128)(2,1)S(1)}, bf16[256,136]{1,0:T(8,128)(2,1)S(1)}, bf16[136,128]{1,0:T(8,128)(2...) custom-call(bf16[136,4096]{1,0:T(8,128)(2,1)} %passages_hbm.1, bf16[32,4096]{1,0:T(8,128)(2,1)} %own_hbm.1, ...), custom_call_target="tpu_custom_call" | custom-call | flops 34816 | bytes 1376256 | tf_op jit(solution)/shard_map/pallas_call | solution.py:207
  2.5 0.0 collective-permute-done.refs_1_
  2.5 0.7 %shard_map.69 = bf16[256,256]{1,0:T(8,128)(2,1)S(1)} custom-call(bf16[136,4096]{1,0:T(8,128)(2,1)S(1)} %get-tuple-element.12.passages_ref, bf16[256,136]{1,0:T(8,128)(2,1)S(1)} %get-tuple-element.13.place_ref, bf16[136,128]{1,0:T(8,128)(2,1)S(1)} %get-tuple-element.14.ids_ref, bf16[32,4096]{1,0:T(8,128)(2,1)S(1)} %get-tuple-element.15.refs_0_, ...), custom_call_target="tpu_custom_call" | custom-call | tf_op jit(solution)/shard_map/pallas_call | solution.py:236
  3.3 15.8 %all_to_all.22 = bf16[16,16,256]{2,1,0:T(8,128)(2,1)S(1)} all-to-all(bf16[16,16,256]{2,1,0:T(8,128)(2,1)S(1)} %bitcast.10), channel_id=1, replica_groups=mesh['doc'=16,'qry'=2] {'doc'}, dimensions={0} | all-to-all | bytes 262144 | tf_op jit(solution)/shard_map/all_to_all | solution.py:241
  19.1 0.6 %shard_map.70 = (f32[16,64]{1,0:T(8,128)S(1)}, f32[32,128]{1,0:T(8,128)S(1)}) custom-call(bf16[256,256]{1,0:T(8,128)(2,1)S(1)} %bitcast.11, f32[16,64]{1,0:T(8,128)S(1)} %get-tuple-element.16.weights_ref, f32[8,64]{1,0:T(8,128)S(1)} %get-tuple-element.17.notes_ref), custom_call_target="tpu_custom_call" | custom-call | tf_op jit(solution)/shard_map/pallas_call | solution.py:243
  19.7 9.1 %all_to_all.23 = f32[32,1,128]{2,1,0:T(1,128)S(1)} all-to-all(f32[32,1,128]{2,1,0:T(1,128)S(1)} %bitcast.13), channel_id=1, replica_groups=mesh['doc'=16,'qry'=2] {'doc','qry'}, dimensions={0} | all-to-all | bytes 32768 | tf_op jit(solution)/shard_map/all_to_all | solution.py:248
  28.8 0.7 %shard_map.71 = (f32[1,32]{1,0:T(1,128)}, f32[16,64]{1,0:T(8,128)}) custom-call(f32[32,128]{1,0:T(8,128)S(1)} %bitcast.12, f32[16,64]{1,0:T(8,128)S(1)} %get-tuple-element.19.scores_in_ref), custom_call_target="tpu_custom_call" | custom-call | tf_op jit(solution)/shard_map/pallas_call | solution.py:249
Async XLA Ops:
  0.6 1.9 %collective-permute-start = (bf16[32,4096]{1,0:T(8,128)(2,1)}, bf16[32,4096]{1,0:T(8,128)(2,1)S(1)}, u32[]{:S(2)}, u32[]{:S(2)}) collective-permute-start(bf16[32,4096]{1,0:T(8,128)(2,1)} %own_hbm.1), channel_id=1, source_target_pairs={{1,0},{0,1},{3,2},{2,3},{5,4},{4,5},{7,6},{6,7},{9,8},{8,9},{11,10... | collective-permute-start | bytes 786440 | tf_op jit(solution)/shard_map/ppermute | solution.py:204

commit v4 on v3

--- a/solution.py
+++ b/solution.py
@@ -13,10 +13,24 @@
 
 score_scale = 0.03125
 very_negative = -1e30
+tiny = 1e-30
+
+STEPS = 10.0
+LEVELS = 2.0 * STEPS + 1.0
+STEP = 256.0 * STEPS
 
 VMEM = pl.BlockSpec(memory_space=pltpu.VMEM)
 HBM = pl.BlockSpec(memory_space=pltpu.HBM)
 NT = (((1,), (1,)), ((), ()))
+
+
+def turned(index, turn, size):
+    index = index + turn % size
+    return jnp.where(index >= size, index - size, index)
+
+
+def turned_group(turn, size):
+    return [[(k + turn) % size for k in range(size)]]
 
 
 def dot_nt(a, b):
@@ -28,7 +42,7 @@
     passages_ref, own_ref, place_ref, ids_ref, weights_ref, notes_ref,
     route_ref, pattern_ref, teacher_ref, passages_sem, small_sem,
 ):
-    doc_count, query_groups, capacity, table_rows, rows_dev = sizes
+    doc_count, query_groups, capacity, table_rows, rows_dev, route_turn = sizes
     rows = passages_ref.shape[0]
     pairs = [
         (route_hbm, route_ref),
@@ -51,7 +65,7 @@
     small[0].wait()
     route = route_ref[...]
     owner = route // table_rows
-    target = (owner // query_groups).astype(jnp.float32)
+    target = turned(owner // query_groups, -route_turn, doc_count).astype(jnp.float32)
     slot = (route - owner * table_rows).astype(jnp.float32)
     down = lax.broadcasted_iota(jnp.int32, (rows, rows), 0)
     across = lax.broadcasted_iota(jnp.int32, (rows, rows), 1)
@@ -97,11 +111,19 @@
     query_refs, out_ref = refs[:-1], refs[-1]
     queries = jnp.concatenate([part[...] for part in query_refs], axis=0)
     logits = dot_nt(passages_ref[...], queries) * score_scale
+    count = logits.shape[1]
     high = logits.astype(jnp.bfloat16)
-    low = (logits - high.astype(jnp.float32)).astype(jnp.bfloat16)
-    columns = jnp.concatenate([high, low, ids_ref[...]], axis=1)
+    rounded = high.astype(jnp.float32)
+    low = logits - rounded
+    inverse = pltpu.reciprocal(jnp.maximum(jnp.abs(rounded), tiny), approx=True)
+    steps = jnp.floor(low * inverse * STEP + 0.5)
+    steps = jnp.clip(steps, -STEPS, STEPS)
+    shared = steps * LEVELS + jnp.concatenate([steps[:, 1:], steps[:, :1]], axis=1)
+    lane = lax.broadcasted_iota(jnp.int32, logits.shape, 1)
+    low = jnp.where(lane == count - 2, shared, low).astype(jnp.bfloat16)
+    low = jnp.where(lane == count - 1, ids_ref[...], low)
     out_ref[...] = jnp.dot(
-        place_ref[...], columns, preferred_element_type=jnp.float32
+        place_ref[...], jnp.concatenate([high, low], axis=1), preferred_element_type=jnp.float32
     ).astype(out_ref.dtype)
 
 
@@ -109,14 +131,21 @@
     doc_dev, all_queries = weights_ref.shape
     table_rows = doc_dev * MAXP
     slots = arrived_ref.shape[0]
-    first = jnp.where(lax.broadcasted_iota(jnp.int32, (SUBLANES, LANES), 1) == 0, 1.0, 0.0)
-    id_row = dot_nt(first.astype(jnp.bfloat16), arrived_ref[:, 2 * all_queries :])[:1]
+    columns = 2 * all_queries
+    last = lax.broadcasted_iota(jnp.int32, (SUBLANES, columns), 1) == columns - 1
+    last = jnp.where(last, 1.0, 0.0).astype(jnp.bfloat16)
+    id_row = dot_nt(last, arrived_ref[...])[:1]
     shape = (MAXP, doc_dev, slots)
     wanted = lax.broadcasted_iota(jnp.int32, shape, 0) + lax.broadcasted_iota(jnp.int32, shape, 1) * MAXP
     wanted = wanted.reshape(table_rows, slots).astype(jnp.float32) + 1.0
     chosen = jnp.where(wanted == id_row, 1.0, 0.0).astype(jnp.bfloat16)
-    table = jnp.dot(chosen, arrived_ref[:, : 2 * all_queries], preferred_element_type=jnp.float32)
-    scores = table[:, :all_queries] + table[:, all_queries:]
+    table = jnp.dot(chosen, arrived_ref[...], preferred_element_type=jnp.float32)
+    high, low = table[:, :all_queries], table[:, all_queries:]
+    lane = lax.broadcasted_iota(jnp.int32, low.shape, 1)
+    shared = jnp.where(lane == all_queries - 1, table[:, all_queries - 1 : columns - 1], low)
+    steps = jnp.floor(shared * (1.0 / LEVELS) + 0.5)
+    steps = jnp.where(lane == all_queries - 1, shared - LEVELS * steps, steps)
+    scores = high + jnp.where(lane >= all_queries - 2, steps * jnp.abs(high) * (1.0 / STEP), low)
     document = lax.broadcasted_iota(jnp.int32, (doc_dev, slots), 0).astype(jnp.float32)
     held = jnp.floor((id_row - 1.0) * (1.0 / MAXP)) == document
     count = jnp.sum(jnp.where(held, 1.0, 0.0), axis=1, keepdims=True)
@@ -131,8 +160,8 @@
         ordered = pooled
         for mine in range(1, query_groups):
             cut = all_queries - mine * rows_dev
-            turned = jnp.concatenate([pooled[:, cut:], pooled[:, :cut]], axis=1)
-            ordered = jnp.where(core == float(mine), turned, ordered)
+            shifted = jnp.concatenate([pooled[:, cut:], pooled[:, :cut]], axis=1)
+            ordered = jnp.where(core == float(mine), shifted, ordered)
         pooled = ordered
     active = notes_ref[2:3, :] > 0.0
     scores_ref[...] = jnp.where(active, pooled, 0.0)
@@ -197,6 +226,7 @@
     all_queries, doc_dev = teacher.shape
     table_rows = doc_dev * MAXP
     capacity = (table_rows + doc_count - 1) // doc_count
+    route_turn = doc_count // 4
     f32, bf16 = jnp.float32, jnp.bfloat16
     shaped = jax.ShapeDtypeStruct
 
@@ -206,13 +236,14 @@
     ]
     held, own, place, ids, weights, notes = call(
         functools.partial(
-            before_kernel, (doc_count, query_groups, capacity, table_rows, rows_dev)
+            before_kernel,
+            (doc_count, query_groups, capacity, table_rows, rows_dev, route_turn),
         ),
         [
             shaped((rows, width), bf16),
             shaped((rows_dev, width), bf16),
             shaped((doc_count * capacity, rows), bf16),
-            shaped((rows, LANES), bf16),
+            shaped((rows, all_queries), bf16),
             shaped((doc_dev, all_queries), f32),
             shaped((SUBLANES, all_queries), f32),
         ],
@@ -235,10 +266,17 @@
     )
     outgoing = call(
         pack_kernel,
-        shaped((doc_count * capacity, 2 * all_queries + LANES), bf16),
+        shaped((doc_count * capacity, 2 * all_queries), bf16),
         [VMEM] * (4 + len(others)),
     )(held, place, ids, own, *others)
-    arrived = lax.all_to_all(outgoing, "doc", split_axis=0, concat_axis=0, tiled=True)
+    arrived = lax.all_to_all(
+        outgoing,
+        "doc",
+        split_axis=0,
+        concat_axis=0,
+        axis_index_groups=turned_group(route_turn, doc_count),
+        tiled=True,
+    )
     line = -(-3 * rows_dev // LANES) * LANES
     doc_scores, partials = call(
         functools.partial(pool_kernel, rows_dev, query_groups),

time: 29.7 us -> 28.6 us (0.963)
  blocking collectives: 24.9 us -> 23.7 us
    all_to_all x1, blocking collectives: 15.8 us -> 14.6 us  [on_device(): lax.all_to_all(outgoing, 'doc', split_axis=0, concat_axis=0, axis_index_g...]
where the time goes in v4:
time: 28.6 us; the launch traced here: 28.4 us
  blocking collectives  23.7 us (83%)
  Pallas kernels  3.51 us (12%)
  between operations  0.66 us (2%)
  starting transfers between devices  0.52 us (2%)
    all_to_all x1, blocking collectives, on_device(): lax.all_to_all(outgoing, 'doc', split_axis=0, concat_axis=0, axis_index_g...  14.6 us
    all_to_all x1, blocking collectives, on_device(): lax.all_to_all(partials, ('doc', 'qry'), split_axis=0, concat_axis=0, til...  9.06 us
    pallas_call x1, Pallas kernels, on_device(): call(functools.partial(before_kernel, (doc_count, query_groups, capacity,...  1.38 us
    pallas_call x1, Pallas kernels, on_device(): call(pack_kernel, shaped((doc_count * capacity, 2 * all_queries), bf16),...  0.82 us
    pallas_call x1, Pallas kernels, on_device(): call(functools.partial(merge_kernel, rows_dev), [shaped((1, rows_dev), f3...  0.69 us
    pallas_call x1, Pallas kernels, on_device(): call(functools.partial(pool_kernel, rows_dev, query_groups), [shaped((doc...  0.62 us
  transfers between devices with their start and end apart: 1, of which 0 were waited for; matrix products, arithmetic and copies ran while one was open for 0% of the time, Pallas kernels for 5%

profile of v4, /device:TPU:0, one launch (start us, length us, event | category | flops | bytes accessed | tf_op | source)
XLA Modules:
  0.0 28.4 jit_solution(1249448433194904362)
XLA Ops:
  0.6 0.5 %collective-permute-start = (bf16[32,4096]{1,0:T(8,128)(2,1)}, bf16[32,4096]{1,0:T(8,128)(2,1)S(1)}, u32[]{:S(2)}, u32[]{:S(2)}) collective-permute-start(bf16[32,4096]{1,0:T(8,128)(2,1)} %own_hbm.1), channel_id=1, source_target_pairs={{1,0},{0,1},{3,2},{2,3},{5,4},{4,5},{7,6},{6,7},{9,8},{8,9},{11,10... | collective-permute-start | bytes 786440 | tf_op jit(solution)/shard_map/ppermute | solution.py:234
  1.1 1.4 %shard_map.68 = (bf16[136,4096]{1,0:T(8,128)(2,1)S(1)}, bf16[32,4096]{1,0:T(8,128)(2,1)S(1)}, bf16[256,136]{1,0:T(8,128)(2,1)S(1)}, bf16[136,64]{1,0:T(8,128)(2,...) custom-call(bf16[136,4096]{1,0:T(8,128)(2,1)} %passages_hbm.1, bf16[32,4096]{1,0:T(8,128)(2,1)} %own_hbm.1, ...), custom_call_target="tpu_custom_call" | custom-call | flops 34816 | bytes 1376256 | tf_op jit(solution)/shard_map/pallas_call | solution.py:237
  2.5 0.0 collective-permute-done.refs_1_
  2.5 0.8 %shard_map.69 = bf16[256,128]{1,0:T(8,128)(2,1)S(1)} custom-call(bf16[136,4096]{1,0:T(8,128)(2,1)S(1)} %get-tuple-element.12.passages_ref, bf16[256,136]{1,0:T(8,128)(2,1)S(1)} %get-tuple-element.13.place_ref, bf16[136,64]{1,0:T(8,128)(2,1)S(1)} %get-tuple-element.14.ids_ref, bf16[32,4096]{1,0:T(8,128)(2,1)S(1)} %get-tuple-element.15.refs_0_, ...), custom_call_target="tpu_custom_call" | custom-call | tf_op jit(solution)/shard_map/pallas_call | solution.py:267
  3.4 14.6 %all_to_all.22 = bf16[16,16,128]{2,1,0:T(8,128)(2,1)S(1)} all-to-all(bf16[16,16,128]{2,1,0:T(8,128)(2,1)S(1)} %bitcast.10), channel_id=1, replica_groups={{8,10,12,14,16,18,20,22,24,26,28,30,0,2,4,6},{9,11,13,15,17,19,21,23,25..., dimensions={0} | all-to-all | bytes 131072 | tf_op jit(solution)/shard_map/all_to_all | solution.py:272
  18.0 0.6 %shard_map.70 = (f32[16,64]{1,0:T(8,128)S(1)}, f32[32,128]{1,0:T(8,128)S(1)}) custom-call(bf16[256,128]{1,0:T(8,128)(2,1)S(1)} %bitcast.11, f32[16,64]{1,0:T(8,128)S(1)} %get-tuple-element.16.weights_ref, f32[8,64]{1,0:T(8,128)S(1)} %get-tuple-element.17.notes_ref), custom_call_target="tpu_custom_call" | custom-call | tf_op jit(solution)/shard_map/pallas_call | solution.py:281
  18.6 9.1 %all_to_all.23 = f32[32,1,128]{2,1,0:T(1,128)S(1)} all-to-all(f32[32,1,128]{2,1,0:T(1,128)S(1)} %bitcast.13), channel_id=1, replica_groups=mesh['doc'=16,'qry'=2] {'doc','qry'}, dimensions={0} | all-to-all | bytes 32768 | tf_op jit(solution)/shard_map/all_to_all | solution.py:286
  27.7 0.7 %shard_map.71 = (f32[1,32]{1,0:T(1,128)}, f32[16,64]{1,0:T(8,128)}) custom-call(f32[32,128]{1,0:T(8,128)S(1)} %bitcast.12, f32[16,64]{1,0:T(8,128)S(1)} %get-tuple-element.19.scores_in_ref), custom_call_target="tpu_custom_call" | custom-call | tf_op jit(solution)/shard_map/pallas_call | solution.py:287
Async XLA Ops:
  0.6 1.9 %collective-permute-start = (bf16[32,4096]{1,0:T(8,128)(2,1)}, bf16[32,4096]{1,0:T(8,128)(2,1)S(1)}, u32[]{:S(2)}, u32[]{:S(2)}) collective-permute-start(bf16[32,4096]{1,0:T(8,128)(2,1)} %own_hbm.1), channel_id=1, source_target_pairs={{1,0},{0,1},{3,2},{2,3},{5,4},{4,5},{7,6},{6,7},{9,8},{8,9},{11,10... | collective-permute-start | bytes 786440 | tf_op jit(solution)/shard_map/ppermute | solution.py:234

commit v5 on v4

--- a/solution.py
+++ b/solution.py
@@ -31,6 +31,26 @@
 
 def turned_group(turn, size):
     return [[(k + turn) % size for k in range(size)]]
+
+
+def rolled(array, columns):
+    if columns == 0:
+        return array
+    return jnp.concatenate([array[:, columns:], array[:, :columns]], axis=1)
+
+
+def from_own(array, core, rows_dev, query_groups):
+    out = array
+    for mine in range(1, query_groups):
+        out = jnp.where(core == mine, rolled(array, mine * rows_dev), out)
+    return out
+
+
+def from_first(array, core, rows_dev, query_groups):
+    out = array
+    for mine in range(1, query_groups):
+        out = jnp.where(core == mine, rolled(array, (query_groups - mine) * rows_dev), out)
+    return out
 
 
 def dot_nt(a, b):
@@ -92,7 +112,8 @@
         inside = (lane >= block * rows_dev) & (lane < (block + 1) * rows_dev)
         flag = jnp.broadcast_to(flags[block : block + 1], (1, all_queries))
         active = jnp.where(inside & (flag > 0), 1.0, active)
-    teacher = teacher_ref[...]
+    active = from_own(active, core, rows_dev, query_groups)
+    teacher = from_own(teacher_ref[...], core, rows_dev, query_groups)
     peak = jnp.max(teacher, axis=0, keepdims=True)
     weights = jnp.exp(teacher - peak)
     weight_sum = jnp.sum(weights, axis=0, keepdims=True)
@@ -101,8 +122,7 @@
     notes_ref[0:1, :] = jnp.where(active > 0.0, peak + jnp.log(weight_sum), very_negative)
     notes_ref[1:2, :] = jnp.sum(weights * teacher, axis=0, keepdims=True)
     notes_ref[2:3, :] = active
-    notes_ref[3:4, :] = jnp.full((1, all_queries), core, jnp.int32).astype(jnp.float32)
-    notes_ref[4:, :] = jnp.zeros((notes_ref.shape[0] - 4, all_queries), jnp.float32)
+    notes_ref[3:, :] = jnp.zeros((notes_ref.shape[0] - 3, all_queries), jnp.float32)
     small[3].wait()
     large.wait()
 
@@ -127,7 +147,7 @@
     ).astype(out_ref.dtype)
 
 
-def pool_kernel(rows_dev, query_groups, arrived_ref, weights_ref, notes_ref, scores_ref, out_ref):
+def pool_kernel(rows_dev, query_groups, arrived_ref, weights_ref, notes_ref, scores_ref, lines_ref):
     doc_dev, all_queries = weights_ref.shape
     table_rows = doc_dev * MAXP
     slots = arrived_ref.shape[0]
@@ -155,14 +175,6 @@
     highest = functools.reduce(jnp.maximum, places)
     total = functools.reduce(jnp.add, [jnp.exp(place - highest) for place in places])
     pooled = highest + jnp.log(total)
-    if query_groups > 1:
-        core = notes_ref[3:4, :]
-        ordered = pooled
-        for mine in range(1, query_groups):
-            cut = all_queries - mine * rows_dev
-            shifted = jnp.concatenate([pooled[:, cut:], pooled[:, :cut]], axis=1)
-            ordered = jnp.where(core == float(mine), shifted, ordered)
-        pooled = ordered
     active = notes_ref[2:3, :] > 0.0
     scores_ref[...] = jnp.where(active, pooled, 0.0)
     peak = jnp.max(pooled, axis=0, keepdims=True)
@@ -170,8 +182,8 @@
     student = jnp.where(active, student, very_negative)
     mean = notes_ref[1:2, :] - jnp.sum(weights_ref[...] * pooled, axis=0, keepdims=True)
     teacher = notes_ref[0:1, :]
-    group = lax.broadcasted_iota(jnp.int32, out_ref.shape, 0) % query_groups
-    out = jnp.zeros(out_ref.shape, jnp.float32)
+    row = lax.broadcasted_iota(jnp.int32, lines_ref.shape, 0)
+    lines = jnp.zeros(lines_ref.shape, jnp.float32)
     for block in range(query_groups):
         part = slice(block * rows_dev, (block + 1) * rows_dev)
         line = jnp.concatenate(
@@ -179,16 +191,31 @@
                 student[:, part],
                 teacher[:, part],
                 mean[:, part],
-                jnp.zeros((1, out_ref.shape[1] - 3 * rows_dev), jnp.float32),
+                jnp.zeros((1, lines_ref.shape[1] - 3 * rows_dev), jnp.float32),
             ],
             axis=1,
         )
-        out = jnp.where(group == block, jnp.broadcast_to(line, out_ref.shape), out)
+        lines = jnp.where(row == block, jnp.broadcast_to(line, lines_ref.shape), lines)
+    lines_ref[...] = lines
+
+
+def order_kernel(rows_dev, query_groups, scores_ref, out_ref):
+    out_ref[...] = from_first(scores_ref[...], lax.axis_index("qry"), rows_dev, query_groups)
+
+
+def spread_kernel(*refs):
+    line_refs, out_ref = refs[:-1], refs[-1]
+    sources = len(line_refs)
+    source = lax.broadcasted_iota(jnp.int32, out_ref.shape, 0) % sources
+    out = jnp.zeros(out_ref.shape, jnp.float32)
+    for k, lines in enumerate(line_refs):
+        part = (sources - k) % sources
+        line = jnp.broadcast_to(lines[part : part + 1, :], out_ref.shape)
+        out = jnp.where(source == k, line, out)
     out_ref[...] = out
 
 
-def merge_kernel(rows_dev, parts_ref, scores_in_ref, out_ref, scores_ref):
-    scores_ref[...] = scores_in_ref[...]
+def merge_kernel(rows_dev, parts_ref, out_ref):
     parts = parts_ref[...]
     student = parts[:, :rows_dev]
     teacher = parts[:, rows_dev : 2 * rows_dev]
@@ -217,6 +244,13 @@
     )
 
 
+def from_others(array, query_groups):
+    return [
+        lax.ppermute(array, "qry", [((i + k) % query_groups, i) for i in range(query_groups)])
+        for k in range(1, query_groups)
+    ]
+
+
 def on_device(queries, passages, passage_route, pattern, teacher):
     doc_count = lax.axis_size("doc")
     query_groups = lax.axis_size("qry")
@@ -226,14 +260,12 @@
     all_queries, doc_dev = teacher.shape
     table_rows = doc_dev * MAXP
     capacity = (table_rows + doc_count - 1) // doc_count
-    route_turn = doc_count // 4
+    route_turn = doc_count - 1
+    total_turn = doc_count - 1
     f32, bf16 = jnp.float32, jnp.bfloat16
     shaped = jax.ShapeDtypeStruct
 
-    others = [
-        lax.ppermute(queries, "qry", [((i + k) % query_groups, i) for i in range(query_groups)])
-        for k in range(1, query_groups)
-    ]
+    others = from_others(queries, query_groups)
     held, own, place, ids, weights, notes = call(
         functools.partial(
             before_kernel,
@@ -278,17 +310,33 @@
         tiled=True,
     )
     line = -(-3 * rows_dev // LANES) * LANES
-    doc_scores, partials = call(
+    lines_rows = -(-query_groups // SUBLANES) * SUBLANES
+    doc_scores, lines = call(
         functools.partial(pool_kernel, rows_dev, query_groups),
-        [shaped((doc_dev, all_queries), f32), shaped((devices, line), f32)],
+        [shaped((doc_dev, all_queries), f32), shaped((lines_rows, line), f32)],
         [VMEM, VMEM, VMEM],
     )(arrived, weights, notes)
-    everyone = lax.all_to_all(partials, ("doc", "qry"), split_axis=0, concat_axis=0, tiled=True)
-    divergence, doc_scores = call(
-        functools.partial(merge_kernel, rows_dev),
-        [shaped((1, rows_dev), f32), shaped((doc_dev, all_queries), f32)],
-        [VMEM, VMEM],
-    )(everyone, doc_scores)
+    received = from_others(lines, query_groups)
+    doc_scores = call(
+        functools.partial(order_kernel, rows_dev, query_groups),
+        shaped((doc_dev, all_queries), f32),
+        [VMEM],
+    )(doc_scores)
+    doc_scores, received = lax.optimization_barrier((doc_scores, received))
+    partials = call(spread_kernel, shaped((devices, line), f32), [VMEM] * query_groups)(
+        lines, *received
+    )
+    everyone = lax.all_to_all(
+        partials,
+        "doc",
+        split_axis=0,
+        concat_axis=0,
+        axis_index_groups=turned_group(total_turn, doc_count),
+        tiled=True,
+    )
+    divergence = call(
+        functools.partial(merge_kernel, rows_dev), shaped((1, rows_dev), f32), [VMEM]
+    )(everyone)
     return (doc_scores.T, divergence.reshape(rows_dev))
 
 

time: 28.6 us -> 28.1 us (0.983)
  blocking collectives: 23.7 us -> 22 us
  Pallas kernels: 3.51 us -> 4.11 us
  waiting for transfers between devices: 0.01 us -> 0.49 us
    all_to_all x1, blocking collectives: 14.6 us -> 12.2 us  [on_device(): lax.all_to_all(outgoing, 'doc', split_axis=0, concat_axis=0, axis_index_g...]
    all_to_all x1, blocking collectives: 9.06 us -> 9.87 us  [on_device(): lax.all_to_all(partials, 'doc', split_axis=0, concat_axis=0, axis_index_g...]
    pallas_call x1 -> x3, Pallas kernels: 0.69 us -> 1.36 us  [the longest x1 0.68 us: on_device(): call(functools.partial(merge_kernel, rows_dev), shaped((1, rows_dev), f32...]
    ppermute x1 -> x2, waiting for transfers between devices: 0.01 us -> 0.49 us  [from_others(): lax.ppermute(array, 'qry', [((i + k) % query_groups, i) for i in range(qu...]
  transfers between devices with their start and end apart: 1 -> 2, of which waited for: 0 -> 1; matrix products, arithmetic and copies ran while one was open for 0% -> 0% of each run, Pallas kernels for 5% -> 7%
where the time goes in v5:
time: 28.1 us; the launch traced here: 27.8 us
  blocking collectives  22 us (78%)
  Pallas kernels  4.11 us (15%)
  between operations  0.67 us (2%)
  starting transfers between devices  0.54 us (2%)
  waiting for transfers between devices  0.49 us (2%)
    all_to_all x1, blocking collectives, on_device(): lax.all_to_all(outgoing, 'doc', split_axis=0, concat_axis=0, axis_index_g...  12.2 us
    all_to_all x1, blocking collectives, on_device(): lax.all_to_all(partials, 'doc', split_axis=0, concat_axis=0, axis_index_g...  9.87 us
    pallas_call x1, Pallas kernels, on_device(): call(functools.partial(before_kernel, (doc_count, query_groups, capacity,...  1.38 us
    pallas_call x1, Pallas kernels, on_device(): call(pack_kernel, shaped((doc_count * capacity, 2 * all_queries), bf16),...  0.82 us
    pallas_call x1, Pallas kernels, on_device(): call(functools.partial(merge_kernel, rows_dev), shaped((1, rows_dev), f32...  0.68 us
    pallas_call x1, Pallas kernels, on_device(): call(functools.partial(order_kernel, rows_dev, query_groups), shaped((doc...  0.67 us
  transfers between devices with their start and end apart: 2, of which 1 were waited for; matrix products, arithmetic and copies ran while one was open for 0% of the time, Pallas kernels for 7%

profile of v5, /device:TPU:0, one launch (start us, length us, event | category | flops | bytes accessed | tf_op | source)
XLA Modules:
  0.0 27.8 jit_solution(6648565108641646316)
XLA Ops:
  0.6 0.5 %collective-permute-start = (bf16[32,4096]{1,0:T(8,128)(2,1)}, bf16[32,4096]{1,0:T(8,128)(2,1)S(1)}, u32[]{:S(2)}, u32[]{:S(2)}) collective-permute-start(bf16[32,4096]{1,0:T(8,128)(2,1)} %own_hbm.1), channel_id=1, source_target_pairs={{1,0},{0,1},{3,2},{2,3},{5,4},{4,5},{7,6},{6,7},{9,8},{8,9},{11,10... | collective-permute-start | bytes 786440 | tf_op jit(solution)/shard_map/ppermute | solution.py:249
  1.1 1.4 %shard_map.68 = (bf16[136,4096]{1,0:T(8,128)(2,1)S(1)}, bf16[32,4096]{1,0:T(8,128)(2,1)S(1)}, bf16[256,136]{1,0:T(8,128)(2,1)S(1)}, bf16[136,64]{1,0:T(8,128)(2,...) custom-call(bf16[136,4096]{1,0:T(8,128)(2,1)} %passages_hbm.1, bf16[32,4096]{1,0:T(8,128)(2,1)} %own_hbm.1, ...), custom_call_target="tpu_custom_call" | custom-call | flops 34816 | bytes 1376256 | tf_op jit(solution)/shard_map/pallas_call | solution.py:269
  2.5 0.0 collective-permute-done.refs_1_
  2.5 0.8 %shard_map.69 = bf16[256,128]{1,0:T(8,128)(2,1)S(1)} custom-call(bf16[136,4096]{1,0:T(8,128)(2,1)S(1)} %get-tuple-element.12.passages_ref, bf16[256,136]{1,0:T(8,128)(2,1)S(1)} %get-tuple-element.13.place_ref, bf16[136,64]{1,0:T(8,128)(2,1)S(1)} %get-tuple-element.14.ids_ref, bf16[32,4096]{1,0:T(8,128)(2,1)S(1)} %get-tuple-element.15.refs_0_, ...), custom_call_target="tpu_custom_call" | custom-call | tf_op jit(solution)/shard_map/pallas_call | solution.py:299
  3.4 12.2 %all_to_all.22 = bf16[16,16,128]{2,1,0:T(8,128)(2,1)S(1)} all-to-all(bf16[16,16,128]{2,1,0:T(8,128)(2,1)S(1)} %bitcast.8), channel_id=1, replica_groups={{30,0,2,4,6,8,10,12,14,16,18,20,22,24,26,28},{31,1,3,5,7,9,11,13,15,17,..., dimensions={0} | all-to-all | bytes 131072 | tf_op jit(solution)/shard_map/all_to_all | solution.py:304
  15.5 0.6 %shard_map.70 = (f32[16,64]{1,0:T(8,128)S(1)}, f32[8,128]{1,0:T(8,128)S(1)}) custom-call(bf16[256,128]{1,0:T(8,128)(2,1)S(1)} %bitcast.9, f32[16,64]{1,0:T(8,128)S(1)} %get-tuple-element.16.weights_ref, f32[8,64]{1,0:T(8,128)S(1)} %get-tuple-element.17.notes_ref), custom_call_target="tpu_custom_call" | custom-call | tf_op jit(solution)/shard_map/pallas_call | solution.py:314
  16.1 0.0 collective-permute-start.1
  16.1 0.7 %shard_map.71 = f32[16,64]{1,0:T(8,128)} custom-call(f32[16,64]{1,0:T(8,128)S(1)} %get-tuple-element.18.scores_ref), custom_call_target="tpu_custom_call" | custom-call | tf_op jit(solution)/shard_map/pallas_call | solution.py:320
  16.8 0.5 %collective-permute-done.1.refs_1_ = f32[8,128]{1,0:T(8,128)S(1)} collective-permute-done((f32[8,128]{1,0:T(8,128)S(1)}, f32[8,128]{1,0:T(8,128)S(1)}, u32[]{:S(2)}, u32[]{:S(2)}) %collective-permute-start.1) | collective-permute-done | bytes 4128 | tf_op jit(solution)/shard_map/ppermute | solution.py:249
  17.3 9.9 %all_to_all.23 = f32[16,2,128]{2,1,0:T(2,128)S(1)} all-to-all(f32[16,2,128]{2,1,0:T(2,128)S(1)} %bitcast.10), channel_id=1, replica_groups={{30,0,2,4,6,8,10,12,14,16,18,20,22,24,26,28},{31,1,3,5,7,9,11,13,15,17,..., dimensions={0} | all-to-all | bytes 32768 | tf_op jit(solution)/shard_map/all_to_all | solution.py:329
  27.2 0.7 %shard_map.73 = f32[1,32]{1,0:T(1,128)} custom-call(f32[32,128]{1,0:T(8,128)S(1)} %bitcast.11), custom_call_target="tpu_custom_call" | custom-call | tf_op jit(solution)/shard_map/pallas_call | solution.py:337
  (1 shorter events, 0.0 us)
Async XLA Ops:
  0.6 1.9 %collective-permute-start = (bf16[32,4096]{1,0:T(8,128)(2,1)}, bf16[32,4096]{1,0:T(8,128)(2,1)S(1)}, u32[]{:S(2)}, u32[]{:S(2)}) collective-permute-start(bf16[32,4096]{1,0:T(8,128)(2,1)} %own_hbm.1), channel_id=1, source_target_pairs={{1,0},{0,1},{3,2},{2,3},{5,4},{4,5},{7,6},{6,7},{9,8},{8,9},{11,10... | collective-permute-start | bytes 786440 | tf_op jit(solution)/shard_map/ppermute | solution.py:249
  16.1 1.2 %collective-permute-start.1 = (f32[8,128]{1,0:T(8,128)S(1)}, f32[8,128]{1,0:T(8,128)S(1)}, u32[]{:S(2)}, u32[]{:S(2)}) collective-permute-start(f32[8,128]{1,0:T(8,128)S(1)} %get-tuple-element.19.refs_0_), channel_id=1, source_target_pairs={{1,0},{0,1},{3,2},{2,3},{5,4},{4,5},{7,6},{6,7},{9,8},{8,9},{11,10... | collective-permute-start | bytes 12296 | tf_op jit(solution)/shard_map/ppermute | solution.py:249

commit v6 on v5

--- a/solution.py
+++ b/solution.py
@@ -1,4 +1,5 @@
 import functools
+import random
 
 import jax
 import jax.numpy as jnp
@@ -10,6 +11,7 @@
 MAXP = 16
 LANES = 128
 SUBLANES = 8
+ORDER_SEED = 3
 
 score_scale = 0.03125
 very_negative = -1e30
@@ -24,13 +26,11 @@
 NT = (((1,), (1,)), ((), ()))
 
 
-def turned(index, turn, size):
-    index = index + turn % size
-    return jnp.where(index >= size, index - size, index)
-
-
-def turned_group(turn, size):
-    return [[(k + turn) % size for k in range(size)]]
+def place_in(order, index):
+    out = jnp.zeros(index.shape, jnp.int32)
+    for place, entry in enumerate(order):
+        out = jnp.where(index == entry, place, out)
+    return out
 
 
 def rolled(array, columns):
@@ -62,7 +62,7 @@
     passages_ref, own_ref, place_ref, ids_ref, weights_ref, notes_ref,
     route_ref, pattern_ref, teacher_ref, passages_sem, small_sem,
 ):
-    doc_count, query_groups, capacity, table_rows, rows_dev, route_turn = sizes
+    doc_count, query_groups, capacity, table_rows, rows_dev, order = sizes
     rows = passages_ref.shape[0]
     pairs = [
         (route_hbm, route_ref),
@@ -85,7 +85,7 @@
     small[0].wait()
     route = route_ref[...]
     owner = route // table_rows
-    target = turned(owner // query_groups, -route_turn, doc_count).astype(jnp.float32)
+    target = place_in(order, owner // query_groups).astype(jnp.float32)
     slot = (route - owner * table_rows).astype(jnp.float32)
     down = lax.broadcasted_iota(jnp.int32, (rows, rows), 0)
     across = lax.broadcasted_iota(jnp.int32, (rows, rows), 1)
@@ -203,15 +203,20 @@
     out_ref[...] = from_first(scores_ref[...], lax.axis_index("qry"), rows_dev, query_groups)
 
 
-def spread_kernel(*refs):
+def spread_kernel(first_place, *refs):
     line_refs, out_ref = refs[:-1], refs[-1]
     sources = len(line_refs)
-    source = lax.broadcasted_iota(jnp.int32, out_ref.shape, 0) % sources
+    row = lax.broadcasted_iota(jnp.int32, out_ref.shape, 0)
+    source = row % sources
+    crossed = jnp.where(row // sources == first_place, 1, 0)
+    here = jnp.where(lax.axis_index("doc") == 0, 1, 0)
+    part = (crossed - here + sources) % sources
     out = jnp.zeros(out_ref.shape, jnp.float32)
     for k, lines in enumerate(line_refs):
-        part = (sources - k) % sources
-        line = jnp.broadcast_to(lines[part : part + 1, :], out_ref.shape)
-        out = jnp.where(source == k, line, out)
+        for ahead in range(sources):
+            held = (ahead - k) % sources
+            line = jnp.broadcast_to(lines[held : held + 1, :], out_ref.shape)
+            out = jnp.where((source == k) & (part == ahead), line, out)
     out_ref[...] = out
 
 
@@ -244,6 +249,13 @@
     )
 
 
+def crossed_groups(order, query_groups):
+    return [
+        [doc * query_groups + (core + (doc == 0)) % query_groups for doc in order]
+        for core in range(query_groups)
+    ]
+
+
 def from_others(array, query_groups):
     return [
         lax.ppermute(array, "qry", [((i + k) % query_groups, i) for i in range(query_groups)])
@@ -260,8 +272,8 @@
     all_queries, doc_dev = teacher.shape
     table_rows = doc_dev * MAXP
     capacity = (table_rows + doc_count - 1) // doc_count
-    route_turn = doc_count - 1
-    total_turn = doc_count - 1
+    last_doc = doc_count - 1
+    order = [last_doc] + random.Random(ORDER_SEED).sample(range(last_doc), last_doc)
     f32, bf16 = jnp.float32, jnp.bfloat16
     shaped = jax.ShapeDtypeStruct
 
@@ -269,7 +281,7 @@
     held, own, place, ids, weights, notes = call(
         functools.partial(
             before_kernel,
-            (doc_count, query_groups, capacity, table_rows, rows_dev, route_turn),
+            (doc_count, query_groups, capacity, table_rows, rows_dev, order),
         ),
         [
             shaped((rows, width), bf16),
@@ -306,7 +318,7 @@
         "doc",
         split_axis=0,
         concat_axis=0,
-        axis_index_groups=turned_group(route_turn, doc_count),
+        axis_index_groups=[order],
         tiled=True,
     )
     line = -(-3 * rows_dev // LANES) * LANES
@@ -323,15 +335,17 @@
         [VMEM],
     )(doc_scores)
     doc_scores, received = lax.optimization_barrier((doc_scores, received))
-    partials = call(spread_kernel, shaped((devices, line), f32), [VMEM] * query_groups)(
-        lines, *received
-    )
+    partials = call(
+        functools.partial(spread_kernel, order.index(0)),
+        shaped((devices, line), f32),
+        [VMEM] * query_groups,
+    )(lines, *received)
     everyone = lax.all_to_all(
         partials,
-        "doc",
+        ("doc", "qry"),
         split_axis=0,
         concat_axis=0,
-        axis_index_groups=turned_group(total_turn, doc_count),
+        axis_index_groups=crossed_groups(order, query_groups),
         tiled=True,
     )
     divergence = call(

time: 28.1 us -> 27.1 us (0.964)
  blocking collectives: 22 us -> 20.9 us
    all_to_all x1, blocking collectives: 9.87 us -> 8.66 us  [on_device(): lax.all_to_all(partials, ('doc', 'qry'), split_axis=0, concat_axis=0, axi...]
  transfers between devices with their start and end apart: 2 -> 2, of which waited for: 1 -> 1; matrix products, arithmetic and copies ran while one was open for 0% -> 0% of each run, Pallas kernels for 7% -> 8%
where the time goes in v6:
time: 27.1 us; the launch traced here: 26.7 us
  blocking collectives  20.9 us (77%)
  Pallas kernels  4.13 us (15%)
  between operations  0.67 us (2%)
  starting transfers between devices  0.54 us (2%)
  waiting for transfers between devices  0.49 us (2%)
    all_to_all x1, blocking collectives, on_device(): lax.all_to_all(outgoing, 'doc', split_axis=0, concat_axis=0, axis_index_g...  12.2 us
    all_to_all x1, blocking collectives, on_device(): lax.all_to_all(partials, ('doc', 'qry'), split_axis=0, concat_axis=0, axi...  8.66 us
    pallas_call x1, Pallas kernels, on_device(): call(functools.partial(before_kernel, (doc_count, query_groups, capacity,...  1.38 us
    pallas_call x1, Pallas kernels, on_device(): call(pack_kernel, shaped((doc_count * capacity, 2 * all_queries), bf16),...  0.82 us
    pallas_call x1, Pallas kernels, on_device(): call(functools.partial(merge_kernel, rows_dev), shaped((1, rows_dev), f32...  0.68 us
    pallas_call x1, Pallas kernels, on_device(): call(functools.partial(order_kernel, rows_dev, query_groups), shaped((doc...  0.67 us
    pallas_call x1, Pallas kernels, on_device(): call(functools.partial(pool_kernel, rows_dev, query_groups), [shaped((doc...  0.55 us
  transfers between devices with their start and end apart: 2, of which 1 were waited for; matrix products, arithmetic and copies ran while one was open for 0% of the time, Pallas kernels for 8%

profile of v6, /device:TPU:0, one launch (start us, length us, event | category | flops | bytes accessed | tf_op | source)
XLA Modules:
  0.0 26.7 jit_solution(5788797515340976630)
XLA Ops:
  0.6 0.5 %collective-permute-start = (bf16[32,4096]{1,0:T(8,128)(2,1)}, bf16[32,4096]{1,0:T(8,128)(2,1)S(1)}, u32[]{:S(2)}, u32[]{:S(2)}) collective-permute-start(bf16[32,4096]{1,0:T(8,128)(2,1)} %own_hbm.1), channel_id=1, source_target_pairs={{1,0},{0,1},{3,2},{2,3},{5,4},{4,5},{7,6},{6,7},{9,8},{8,9},{11,10... | collective-permute-start | bytes 786440 | tf_op jit(solution)/shard_map/ppermute | solution.py:261
  1.1 1.4 %shard_map.68 = (bf16[136,4096]{1,0:T(8,128)(2,1)S(1)}, bf16[32,4096]{1,0:T(8,128)(2,1)S(1)}, bf16[256,136]{1,0:T(8,128)(2,1)S(1)}, bf16[136,64]{1,0:T(8,128)(2,...) custom-call(bf16[136,4096]{1,0:T(8,128)(2,1)} %passages_hbm.1, bf16[32,4096]{1,0:T(8,128)(2,1)} %own_hbm.1, ...), custom_call_target="tpu_custom_call" | custom-call | flops 34816 | bytes 1376256 | tf_op jit(solution)/shard_map/pallas_call | solution.py:281
  2.5 0.0 collective-permute-done.refs_1_
  2.5 0.8 %shard_map.69 = bf16[256,128]{1,0:T(8,128)(2,1)S(1)} custom-call(bf16[136,4096]{1,0:T(8,128)(2,1)S(1)} %get-tuple-element.12.passages_ref, bf16[256,136]{1,0:T(8,128)(2,1)S(1)} %get-tuple-element.13.place_ref, bf16[136,64]{1,0:T(8,128)(2,1)S(1)} %get-tuple-element.14.ids_ref, bf16[32,4096]{1,0:T(8,128)(2,1)S(1)} %get-tuple-element.15.refs_0_, ...), custom_call_target="tpu_custom_call" | custom-call | tf_op jit(solution)/shard_map/pallas_call | solution.py:311
  3.4 12.2 %all_to_all.22 = bf16[16,16,128]{2,1,0:T(8,128)(2,1)S(1)} all-to-all(bf16[16,16,128]{2,1,0:T(8,128)(2,1)S(1)} %bitcast.8), channel_id=1, replica_groups={{30,6,18,16,4,10,26,14,2,8,0,28,22,12,20,24},{31,7,19,17,5,11,27,15,3,9..., dimensions={0} | all-to-all | bytes 131072 | tf_op jit(solution)/shard_map/all_to_all | solution.py:316
  15.6 0.6 %shard_map.70 = (f32[16,64]{1,0:T(8,128)S(1)}, f32[8,128]{1,0:T(8,128)S(1)}) custom-call(bf16[256,128]{1,0:T(8,128)(2,1)S(1)} %bitcast.9, f32[16,64]{1,0:T(8,128)S(1)} %get-tuple-element.16.weights_ref, f32[8,64]{1,0:T(8,128)S(1)} %get-tuple-element.17.notes_ref), custom_call_target="tpu_custom_call" | custom-call | tf_op jit(solution)/shard_map/pallas_call | solution.py:326
  16.1 0.0 collective-permute-start.1
  16.2 0.7 %shard_map.71 = f32[16,64]{1,0:T(8,128)} custom-call(f32[16,64]{1,0:T(8,128)S(1)} %get-tuple-element.18.scores_ref), custom_call_target="tpu_custom_call" | custom-call | tf_op jit(solution)/shard_map/pallas_call | solution.py:332
  16.8 0.5 %collective-permute-done.1.refs_1_ = f32[8,128]{1,0:T(8,128)S(1)} collective-permute-done((f32[8,128]{1,0:T(8,128)S(1)}, f32[8,128]{1,0:T(8,128)S(1)}, u32[]{:S(2)}, u32[]{:S(2)}) %collective-permute-start.1) | collective-permute-done | bytes 4128 | tf_op jit(solution)/shard_map/ppermute | solution.py:261
  17.3 8.7 %all_to_all.23 = f32[16,2,128]{2,1,0:T(2,128)S(1)} all-to-all(f32[16,2,128]{2,1,0:T(2,128)S(1)} %bitcast.10), channel_id=1, replica_groups={{30,6,18,16,4,10,26,14,2,8,1,28,22,12,20,24},{31,7,19,17,5,11,27,15,3,9..., dimensions={0} | all-to-all | bytes 32768 | tf_op jit(solution)/shard_map/all_to_all | solution.py:343
  26.0 0.7 %shard_map.73 = f32[1,32]{1,0:T(1,128)} custom-call(f32[32,128]{1,0:T(8,128)S(1)} %bitcast.11), custom_call_target="tpu_custom_call" | custom-call | tf_op jit(solution)/shard_map/pallas_call | solution.py:351
  (1 shorter events, 0.0 us)
Async XLA Ops:
  0.6 1.9 %collective-permute-start = (bf16[32,4096]{1,0:T(8,128)(2,1)}, bf16[32,4096]{1,0:T(8,128)(2,1)S(1)}, u32[]{:S(2)}, u32[]{:S(2)}) collective-permute-start(bf16[32,4096]{1,0:T(8,128)(2,1)} %own_hbm.1), channel_id=1, source_target_pairs={{1,0},{0,1},{3,2},{2,3},{5,4},{4,5},{7,6},{6,7},{9,8},{8,9},{11,10... | collective-permute-start | bytes 786440 | tf_op jit(solution)/shard_map/ppermute | solution.py:261
  16.1 1.2 %collective-permute-start.1 = (f32[8,128]{1,0:T(8,128)S(1)}, f32[8,128]{1,0:T(8,128)S(1)}, u32[]{:S(2)}, u32[]{:S(2)}) collective-permute-start(f32[8,128]{1,0:T(8,128)S(1)} %get-tuple-element.19.refs_0_), channel_id=1, source_target_pairs={{1,0},{0,1},{3,2},{2,3},{5,4},{4,5},{7,6},{6,7},{9,8},{8,9},{11,10... | collective-permute-start | bytes 12296 | tf_op jit(solution)/shard_map/ppermute | solution.py:261

commit v7 on v6

--- a/solution.py
+++ b/solution.py
@@ -11,7 +11,7 @@
 MAXP = 16
 LANES = 128
 SUBLANES = 8
-ORDER_SEED = 3
+ORDER_SEED = 25
 
 score_scale = 0.03125
 very_negative = -1e30
@@ -177,8 +177,8 @@
     pooled = highest + jnp.log(total)
     active = notes_ref[2:3, :] > 0.0
     scores_ref[...] = jnp.where(active, pooled, 0.0)
-    peak = jnp.max(pooled, axis=0, keepdims=True)
-    student = peak + jnp.log(jnp.sum(jnp.exp(pooled - peak), axis=0, keepdims=True))
+    peak = jnp.max(highest, axis=0, keepdims=True)
+    student = peak + jnp.log(jnp.sum(total * jnp.exp(highest - peak), axis=0, keepdims=True))
     student = jnp.where(active, student, very_negative)
     mean = notes_ref[1:2, :] - jnp.sum(weights_ref[...] * pooled, axis=0, keepdims=True)
     teacher = notes_ref[0:1, :]
@@ -222,18 +222,16 @@
 
 def merge_kernel(rows_dev, parts_ref, out_ref):
     parts = parts_ref[...]
-    student = parts[:, :rows_dev]
-    teacher = parts[:, rows_dev : 2 * rows_dev]
-    mean = parts[:, 2 * rows_dev : 3 * rows_dev]
-    peak_student = jnp.max(student, axis=0, keepdims=True)
-    student_total = peak_student + jnp.log(
-        jnp.sum(jnp.exp(student - peak_student), axis=0, keepdims=True)
-    )
-    peak_teacher = jnp.max(teacher, axis=0, keepdims=True)
-    weights = jnp.exp(teacher - peak_teacher)
-    weight_sum = jnp.sum(weights, axis=0, keepdims=True)
-    weighted = jnp.sum(weights * mean, axis=0, keepdims=True) / weight_sum
-    out_ref[...] = weighted - (peak_teacher + jnp.log(weight_sum)) + student_total
+    peak = jnp.max(parts, axis=0, keepdims=True)
+    weights = jnp.exp(parts - peak)
+    total = jnp.sum(weights, axis=0, keepdims=True)
+    moved = jnp.concatenate([weights[:, -rows_dev:], weights[:, :-rows_dev]], axis=1)
+    weighted = jnp.sum(moved * parts, axis=0, keepdims=True)
+    totals = peak + jnp.log(total)
+    columns = [slice(k * rows_dev, (k + 1) * rows_dev) for k in range(3)]
+    out_ref[...] = (
+        weighted[:, columns[2]] / total[:, columns[1]] - totals[:, columns[1]] + totals[:, columns[0]]
+    )
 
 
 def call(kernel, out_shape, in_specs, scratch=(), **cost):
@@ -256,6 +254,11 @@
     ]
 
 
+def shuffled_from(first, size):
+    others = [k for k in range(size) if k != first]
+    return [first] + random.Random(ORDER_SEED).sample(others, size - 1)
+
+
 def from_others(array, query_groups):
     return [
         lax.ppermute(array, "qry", [((i + k) % query_groups, i) for i in range(query_groups)])
@@ -273,7 +276,8 @@
     table_rows = doc_dev * MAXP
     capacity = (table_rows + doc_count - 1) // doc_count
     last_doc = doc_count - 1
-    order = [last_doc] + random.Random(ORDER_SEED).sample(range(last_doc), last_doc)
+    order = shuffled_from(last_doc, doc_count)
+    route_order = shuffled_from(last_doc - doc_count // 4, doc_count)
     f32, bf16 = jnp.float32, jnp.bfloat16
     shaped = jax.ShapeDtypeStruct
 
@@ -281,7 +285,7 @@
     held, own, place, ids, weights, notes = call(
         functools.partial(
             before_kernel,
-            (doc_count, query_groups, capacity, table_rows, rows_dev, order),
+            (doc_count, query_groups, capacity, table_rows, rows_dev, route_order),
         ),
         [
             shaped((rows, width), bf16),
@@ -318,7 +322,7 @@
         "doc",
         split_axis=0,
         concat_axis=0,
-        axis_index_groups=[order],
+        axis_index_groups=[route_order],
         tiled=True,
     )
     line = -(-3 * rows_dev // LANES) * LANES

time: 27.1 us -> 26.5 us (0.978)
  blocking collectives: 20.9 us -> 20.3 us
    all_to_all x1, blocking collectives: 8.66 us -> 8.28 us  [on_device(): lax.all_to_all(partials, ('doc', 'qry'), split_axis=0, concat_axis=0, axi...]
where the time goes in v7:
time: 26.5 us; the launch traced here: 26.1 us
  blocking collectives  20.3 us (77%)
  Pallas kernels  4.12 us (16%)
  between operations  0.67 us (3%)
  starting transfers between devices  0.53 us (2%)
  waiting for transfers between devices  0.48 us (2%)
    all_to_all x1, blocking collectives, on_device(): lax.all_to_all(outgoing, 'doc', split_axis=0, concat_axis=0, axis_index_g...  12 us
    all_to_all x1, blocking collectives, on_device(): lax.all_to_all(partials, ('doc', 'qry'), split_axis=0, concat_axis=0, axi...  8.28 us
    pallas_call x1, Pallas kernels, on_device(): call(functools.partial(before_kernel, (doc_count, query_groups, capacity,...  1.38 us
    pallas_call x1, Pallas kernels, on_device(): call(pack_kernel, shaped((doc_count * capacity, 2 * all_queries), bf16),...  0.82 us
    pallas_call x1, Pallas kernels, on_device(): call(functools.partial(merge_kernel, rows_dev), shaped((1, rows_dev), f32...  0.68 us
    pallas_call x1, Pallas kernels, on_device(): call(functools.partial(order_kernel, rows_dev, query_groups), shaped((doc...  0.67 us
    pallas_call x1, Pallas kernels, on_device(): call(functools.partial(pool_kernel, rows_dev, query_groups), [shaped((doc...  0.54 us
    ppermute x2, starting transfers between devices, from_others(): lax.ppermute(array, 'qry', [((i + k) % query_groups, i) for i in range(qu...  0.53 us
  transfers between devices with their start and end apart: 2, of which 1 were waited for; matrix products, arithmetic and copies ran while one was open for 0% of the time, Pallas kernels for 8%

profile of v7, /device:TPU:0, one launch (start us, length us, event | category | flops | bytes accessed | tf_op | source)
XLA Modules:
  0.0 26.1 jit_solution(11445550066518958441)
XLA Ops:
  0.6 0.5 %collective-permute-start = (bf16[32,4096]{1,0:T(8,128)(2,1)}, bf16[32,4096]{1,0:T(8,128)(2,1)S(1)}, u32[]{:S(2)}, u32[]{:S(2)}) collective-permute-start(bf16[32,4096]{1,0:T(8,128)(2,1)} %own_hbm.1), channel_id=1, source_target_pairs={{1,0},{0,1},{3,2},{2,3},{5,4},{4,5},{7,6},{6,7},{9,8},{8,9},{11,10... | collective-permute-start | bytes 786440 | tf_op jit(solution)/shard_map/ppermute | solution.py:264
  1.1 1.4 %shard_map.68 = (bf16[136,4096]{1,0:T(8,128)(2,1)S(1)}, bf16[32,4096]{1,0:T(8,128)(2,1)S(1)}, bf16[256,136]{1,0:T(8,128)(2,1)S(1)}, bf16[136,64]{1,0:T(8,128)(2,...) custom-call(bf16[136,4096]{1,0:T(8,128)(2,1)} %passages_hbm.1, bf16[32,4096]{1,0:T(8,128)(2,1)} %own_hbm.1, ...), custom_call_target="tpu_custom_call" | custom-call | flops 34816 | bytes 1376256 | tf_op jit(solution)/shard_map/pallas_call | solution.py:285
  2.5 0.0 collective-permute-done.refs_1_
  2.5 0.8 %shard_map.69 = bf16[256,128]{1,0:T(8,128)(2,1)S(1)} custom-call(bf16[136,4096]{1,0:T(8,128)(2,1)S(1)} %get-tuple-element.12.passages_ref, bf16[256,136]{1,0:T(8,128)(2,1)S(1)} %get-tuple-element.13.place_ref, bf16[136,64]{1,0:T(8,128)(2,1)S(1)} %get-tuple-element.14.ids_ref, bf16[32,4096]{1,0:T(8,128)(2,1)S(1)} %get-tuple-element.15.refs_0_, ...), custom_call_target="tpu_custom_call" | custom-call | tf_op jit(solution)/shard_map/pallas_call | solution.py:315
  3.4 12.0 %all_to_all.22 = bf16[16,16,128]{2,1,0:T(8,128)(2,1)S(1)} all-to-all(bf16[16,16,128]{2,1,0:T(8,128)(2,1)S(1)} %bitcast.8), channel_id=1, replica_groups={{22,12,26,0,6,8,14,28,20,16,4,18,24,30,10,2},{23,13,27,1,7,9,15,29,21,1..., dimensions={0} | all-to-all | bytes 131072 | tf_op jit(solution)/shard_map/all_to_all | solution.py:320
  15.4 0.5 %shard_map.70 = (f32[16,64]{1,0:T(8,128)S(1)}, f32[8,128]{1,0:T(8,128)S(1)}) custom-call(bf16[256,128]{1,0:T(8,128)(2,1)S(1)} %bitcast.9, f32[16,64]{1,0:T(8,128)S(1)} %get-tuple-element.16.weights_ref, f32[8,64]{1,0:T(8,128)S(1)} %get-tuple-element.17.notes_ref), custom_call_target="tpu_custom_call" | custom-call | tf_op jit(solution)/shard_map/pallas_call | solution.py:330
  16.0 0.0 collective-permute-start.1
  16.0 0.7 %shard_map.71 = f32[16,64]{1,0:T(8,128)} custom-call(f32[16,64]{1,0:T(8,128)S(1)} %get-tuple-element.18.scores_ref), custom_call_target="tpu_custom_call" | custom-call | tf_op jit(solution)/shard_map/pallas_call | solution.py:336
  16.7 0.5 %collective-permute-done.1.refs_1_ = f32[8,128]{1,0:T(8,128)S(1)} collective-permute-done((f32[8,128]{1,0:T(8,128)S(1)}, f32[8,128]{1,0:T(8,128)S(1)}, u32[]{:S(2)}, u32[]{:S(2)}) %collective-permute-start.1) | collective-permute-done | bytes 4128 | tf_op jit(solution)/shard_map/ppermute | solution.py:264
  17.2 8.3 %all_to_all.23 = f32[16,2,128]{2,1,0:T(2,128)S(1)} all-to-all(f32[16,2,128]{2,1,0:T(2,128)S(1)} %bitcast.10), channel_id=1, replica_groups={{30,12,24,1,6,8,14,26,20,16,4,18,22,28,10,2},{31,13,25,0,7,9,15,27,21,1..., dimensions={0} | all-to-all | bytes 32768 | tf_op jit(solution)/shard_map/all_to_all | solution.py:347
  25.4 0.7 %shard_map.73 = f32[1,32]{1,0:T(1,128)} custom-call(f32[32,128]{1,0:T(8,128)S(1)} %bitcast.11), custom_call_target="tpu_custom_call" | custom-call | tf_op jit(solution)/shard_map/pallas_call | solution.py:355
  (1 shorter events, 0.0 us)
Async XLA Ops:
  0.6 1.9 %collective-permute-start = (bf16[32,4096]{1,0:T(8,128)(2,1)}, bf16[32,4096]{1,0:T(8,128)(2,1)S(1)}, u32[]{:S(2)}, u32[]{:S(2)}) collective-permute-start(bf16[32,4096]{1,0:T(8,128)(2,1)} %own_hbm.1), channel_id=1, source_target_pairs={{1,0},{0,1},{3,2},{2,3},{5,4},{4,5},{7,6},{6,7},{9,8},{8,9},{11,10... | collective-permute-start | bytes 786440 | tf_op jit(solution)/shard_map/ppermute | solution.py:264
  16.0 1.2 %collective-permute-start.1 = (f32[8,128]{1,0:T(8,128)S(1)}, f32[8,128]{1,0:T(8,128)S(1)}, u32[]{:S(2)}, u32[]{:S(2)}) collective-permute-start(f32[8,128]{1,0:T(8,128)S(1)} %get-tuple-element.19.refs_0_), channel_id=1, source_target_pairs={{1,0},{0,1},{3,2},{2,3},{5,4},{4,5},{7,6},{6,7},{9,8},{8,9},{11,10... | collective-permute-start | bytes 12296 | tf_op jit(solution)/shard_map/ppermute | solution.py:264

commit v8 on v7

--- a/solution.py
+++ b/solution.py
@@ -11,15 +11,11 @@
 MAXP = 16
 LANES = 128
 SUBLANES = 8
+PACKED = 16
 ORDER_SEED = 25
 
 score_scale = 0.03125
 very_negative = -1e30
-tiny = 1e-30
-
-STEPS = 10.0
-LEVELS = 2.0 * STEPS + 1.0
-STEP = 256.0 * STEPS
 
 VMEM = pl.BlockSpec(memory_space=pltpu.VMEM)
 HBM = pl.BlockSpec(memory_space=pltpu.HBM)
@@ -99,14 +95,26 @@
     placing = target * capacity + position
     outgoing = lax.broadcasted_iota(jnp.int32, (doc_count * capacity, rows), 0).astype(jnp.float32)
     place_ref[...] = jnp.where(outgoing == placing, 1.0, 0.0).astype(place_ref.dtype)
-    ids_ref[...] = jnp.broadcast_to(as_column(slot) + 1.0, ids_ref.shape).astype(ids_ref.dtype)
+    columns = ids_ref.shape[1]
+    mine = place_in(order, jnp.full((1, 1), lax.axis_index("doc"), jnp.int32)) * capacity
+    arriving = as_column(position) + mine.astype(jnp.float32)
+    number = as_column(slot) + 1.0
+    row = lax.broadcasted_iota(jnp.int32, (ids_ref.shape[0], rows), 0)
+    column = lax.broadcasted_iota(jnp.int32, (rows, columns), 1).astype(jnp.float32)
+    ids = jnp.zeros(ids_ref.shape, jnp.float32)
+    for line in range(-(-doc_count * capacity // columns)):
+        goes = ((row // SUBLANES).astype(jnp.float32) == target) & (row % SUBLANES == line)
+        goes = jnp.where(goes, 1.0, 0.0).astype(jnp.bfloat16)
+        here = jnp.where(column + float(line * columns) == arriving, number, 0.0)
+        ids += jnp.dot(goes, here.astype(jnp.bfloat16), preferred_element_type=jnp.float32)
+    ids_ref[...] = ids
 
     small[1].wait()
     small[2].wait()
     all_queries = rows_dev * query_groups
     lane = lax.broadcasted_iota(jnp.int32, (1, all_queries), 1)
-    mine = lax.broadcasted_iota(jnp.int32, pattern_ref.shape, 1) == group_id
-    flags = jnp.sum(jnp.where(mine, pattern_ref[...], 0), axis=1, keepdims=True)
+    own = lax.broadcasted_iota(jnp.int32, pattern_ref.shape, 1) == group_id
+    flags = jnp.sum(jnp.where(own, pattern_ref[...], 0), axis=1, keepdims=True)
     active = jnp.zeros((1, all_queries), jnp.float32)
     for block in range(query_groups):
         inside = (lane >= block * rows_dev) & (lane < (block + 1) * rows_dev)
@@ -129,43 +137,36 @@
 
 def pack_kernel(passages_ref, place_ref, ids_ref, *refs):
     query_refs, out_ref = refs[:-1], refs[-1]
+    doc_count, block_rows, columns = out_ref.shape
+    capacity = block_rows - SUBLANES
     queries = jnp.concatenate([part[...] for part in query_refs], axis=0)
     logits = dot_nt(passages_ref[...], queries) * score_scale
-    count = logits.shape[1]
     high = logits.astype(jnp.bfloat16)
-    rounded = high.astype(jnp.float32)
-    low = logits - rounded
-    inverse = pltpu.reciprocal(jnp.maximum(jnp.abs(rounded), tiny), approx=True)
-    steps = jnp.floor(low * inverse * STEP + 0.5)
-    steps = jnp.clip(steps, -STEPS, STEPS)
-    shared = steps * LEVELS + jnp.concatenate([steps[:, 1:], steps[:, :1]], axis=1)
-    lane = lax.broadcasted_iota(jnp.int32, logits.shape, 1)
-    low = jnp.where(lane == count - 2, shared, low).astype(jnp.bfloat16)
-    low = jnp.where(lane == count - 1, ids_ref[...], low)
-    out_ref[...] = jnp.dot(
+    low = (logits - high.astype(jnp.float32)).astype(jnp.bfloat16)
+    placed = jnp.dot(
         place_ref[...], jnp.concatenate([high, low], axis=1), preferred_element_type=jnp.float32
-    ).astype(out_ref.dtype)
+    )
+    out_ref[:, :capacity, :] = placed.reshape(doc_count, capacity, columns).astype(out_ref.dtype)
+    ids = ids_ref[...].reshape(doc_count, SUBLANES, columns)
+    out_ref[:, capacity:, :] = ids.astype(out_ref.dtype)
 
 
 def pool_kernel(rows_dev, query_groups, arrived_ref, weights_ref, notes_ref, scores_ref, lines_ref):
     doc_dev, all_queries = weights_ref.shape
     table_rows = doc_dev * MAXP
-    slots = arrived_ref.shape[0]
-    columns = 2 * all_queries
-    last = lax.broadcasted_iota(jnp.int32, (SUBLANES, columns), 1) == columns - 1
-    last = jnp.where(last, 1.0, 0.0).astype(jnp.bfloat16)
-    id_row = dot_nt(last, arrived_ref[...])[:1]
+    doc_count, block_rows, columns = arrived_ref.shape
+    capacity = block_rows - SUBLANES
+    slots = doc_count * capacity
+    ids = jnp.sum(arrived_ref[:, capacity:, :].astype(jnp.float32), axis=0)
+    lines = [ids[line : line + 1] for line in range(-(-slots // columns))]
+    id_row = jnp.concatenate(lines, axis=1)[:, :slots]
     shape = (MAXP, doc_dev, slots)
     wanted = lax.broadcasted_iota(jnp.int32, shape, 0) + lax.broadcasted_iota(jnp.int32, shape, 1) * MAXP
     wanted = wanted.reshape(table_rows, slots).astype(jnp.float32) + 1.0
     chosen = jnp.where(wanted == id_row, 1.0, 0.0).astype(jnp.bfloat16)
-    table = jnp.dot(chosen, arrived_ref[...], preferred_element_type=jnp.float32)
-    high, low = table[:, :all_queries], table[:, all_queries:]
-    lane = lax.broadcasted_iota(jnp.int32, low.shape, 1)
-    shared = jnp.where(lane == all_queries - 1, table[:, all_queries - 1 : columns - 1], low)
-    steps = jnp.floor(shared * (1.0 / LEVELS) + 0.5)
-    steps = jnp.where(lane == all_queries - 1, shared - LEVELS * steps, steps)
-    scores = high + jnp.where(lane >= all_queries - 2, steps * jnp.abs(high) * (1.0 / STEP), low)
+    arrived = arrived_ref[:, :capacity, :].reshape(slots, columns)
+    table = jnp.dot(chosen, arrived, preferred_element_type=jnp.float32)
+    scores = table[:, :all_queries] + table[:, all_queries:]
     document = lax.broadcasted_iota(jnp.int32, (doc_dev, slots), 0).astype(jnp.float32)
     held = jnp.floor((id_row - 1.0) * (1.0 / MAXP)) == document
     count = jnp.sum(jnp.where(held, 1.0, 0.0), axis=1, keepdims=True)
@@ -274,7 +275,7 @@
     rows = passages.shape[0]
     all_queries, doc_dev = teacher.shape
     table_rows = doc_dev * MAXP
-    capacity = (table_rows + doc_count - 1) // doc_count
+    capacity = -(-table_rows // (doc_count * PACKED)) * PACKED
     last_doc = doc_count - 1
     order = shuffled_from(last_doc, doc_count)
     route_order = shuffled_from(last_doc - doc_count // 4, doc_count)
@@ -291,7 +292,7 @@
             shaped((rows, width), bf16),
             shaped((rows_dev, width), bf16),
             shaped((doc_count * capacity, rows), bf16),
-            shaped((rows, all_queries), bf16),
+            shaped((doc_count * SUBLANES, 2 * all_queries), f32),
             shaped((doc_dev, all_queries), f32),
             shaped((SUBLANES, all_queries), f32),
         ],
@@ -314,7 +315,7 @@
     )
     outgoing = call(
         pack_kernel,
-        shaped((doc_count * capacity, 2 * all_queries), bf16),
+        shaped((doc_count, capacity + SUBLANES, 2 * all_queries), bf16),
         [VMEM] * (4 + len(others)),
     )(held, place, ids, own, *others)
     arrived = lax.all_to_all(

time: 26.5 us -> 26.4 us (level)
  no operation moved by 1% of the time
where the time goes in v8:
time: 26.4 us; the launch traced here: 26 us
  blocking collectives  20.5 us (78%)
  Pallas kernels  3.86 us (15%)
  between operations  0.67 us (3%)
  starting transfers between devices  0.53 us (2%)
  waiting for transfers between devices  0.48 us (2%)
    all_to_all x1, blocking collectives, on_device(): lax.all_to_all(outgoing, 'doc', split_axis=0, concat_axis=0, axis_index_g...  12.2 us
    all_to_all x1, blocking collectives, on_device(): lax.all_to_all(partials, ('doc', 'qry'), split_axis=0, concat_axis=0, axi...  8.28 us
    pallas_call x1, Pallas kernels, on_device(): call(functools.partial(before_kernel, (doc_count, query_groups, capacity,...  1.38 us
    pallas_call x1, Pallas kernels, on_device(): call(pack_kernel, shaped((doc_count, capacity + SUBLANES, 2 * all_queries...  0.74 us
    pallas_call x1, Pallas kernels, on_device(): call(functools.partial(merge_kernel, rows_dev), shaped((1, rows_dev), f32...  0.68 us
    pallas_call x1, Pallas kernels, on_device(): call(functools.partial(order_kernel, rows_dev, query_groups), shaped((doc...  0.67 us
    ppermute x2, starting transfers between devices, from_others(): lax.ppermute(array, 'qry', [((i + k) % query_groups, i) for i in range(qu...  0.53 us
  transfers between devices with their start and end apart: 2, of which 1 were waited for; matrix products, arithmetic and copies ran while one was open for 0% of the time, Pallas kernels for 8%

profile of v8, /device:TPU:0, one launch (start us, length us, event | category | flops | bytes accessed | tf_op | source)
XLA Modules:
  0.0 26.0 jit_solution(16720655069361202211)
XLA Ops:
  0.6 0.5 %collective-permute-start = (bf16[32,4096]{1,0:T(8,128)(2,1)}, bf16[32,4096]{1,0:T(8,128)(2,1)S(1)}, u32[]{:S(2)}, u32[]{:S(2)}) collective-permute-start(bf16[32,4096]{1,0:T(8,128)(2,1)} %own_hbm.1), channel_id=1, source_target_pairs={{1,0},{0,1},{3,2},{2,3},{5,4},{4,5},{7,6},{6,7},{9,8},{8,9},{11,10... | collective-permute-start | bytes 786440 | tf_op jit(solution)/shard_map/ppermute | solution.py:265
  1.1 1.4 %shard_map.68 = (bf16[136,4096]{1,0:T(8,128)(2,1)S(1)}, bf16[32,4096]{1,0:T(8,128)(2,1)S(1)}, bf16[256,136]{1,0:T(8,128)(2,1)S(1)}, f32[128,128]{1,0:T(8,128)S(1...) custom-call(bf16[136,4096]{1,0:T(8,128)(2,1)} %passages_hbm.1, bf16[32,4096]{1,0:T(8,128)(2,1)} %own_hbm.1, ...), custom_call_target="tpu_custom_call" | custom-call | flops 34816 | bytes 1376256 | tf_op jit(solution)/shard_map/pallas_call | solution.py:286
  2.5 0.0 collective-permute-done.refs_1_
  2.5 0.7 %shard_map.69 = bf16[16,24,128]{2,1,0:T(8,128)(2,1)S(1)} custom-call(bf16[136,4096]{1,0:T(8,128)(2,1)S(1)} %get-tuple-element.12.passages_ref, bf16[256,136]{1,0:T(8,128)(2,1)S(1)} %get-tuple-element.13.place_ref, f32[128,128]{1,0:T(8,128)S(1)} %get-tuple-element.14.ids_ref, bf16[32,4096]{1,0:T(8,128)(2,1)S(1)} %get-tuple-element.15.refs_0_, ...), custom_call_target="tpu_custom_call" | custom-call | tf_op jit(solution)/shard_map/pallas_call | solution.py:316
  3.3 12.2 %all_to_all.16.arrived_ref = bf16[16,24,128]{2,1,0:T(8,128)(2,1)S(1)} all-to-all(bf16[16,24,128]{2,1,0:T(8,128)(2,1)S(1)} %shard_map.69), channel_id=1, replica_groups={{22,12,26,0,6,8,14,28,20,16,4,18,24,30,10,2},{23,13,27,1,7,9,15,29,21,1..., dimensions={0} | all-to-all | bytes 196608 | tf_op jit(solution)/shard_map/all_to_all | solution.py:321
  15.5 0.4 %shard_map.70 = (f32[16,64]{1,0:T(8,128)S(1)}, f32[8,128]{1,0:T(8,128)S(1)}) custom-call(bf16[16,24,128]{2,1,0:T(8,128)(2,1)S(1)} %all_to_all.16.arrived_ref, f32[16,64]{1,0:T(8,128)S(1)} %get-tuple-element.16.weights_ref, f32[8,64]{1,0:T(8,128)S(1)} %get-tuple-element.17.notes_ref), custom_call_target="tpu_custom_call" | custom-call | tf_op jit(solution)/shard_map/pallas_call | solution.py:331
  15.9 0.0 collective-permute-start.1
  15.9 0.7 %shard_map.71 = f32[16,64]{1,0:T(8,128)} custom-call(f32[16,64]{1,0:T(8,128)S(1)} %get-tuple-element.18.scores_ref), custom_call_target="tpu_custom_call" | custom-call | tf_op jit(solution)/shard_map/pallas_call | solution.py:337
  16.6 0.5 %collective-permute-done.1.refs_1_ = f32[8,128]{1,0:T(8,128)S(1)} collective-permute-done((f32[8,128]{1,0:T(8,128)S(1)}, f32[8,128]{1,0:T(8,128)S(1)}, u32[]{:S(2)}, u32[]{:S(2)}) %collective-permute-start.1) | collective-permute-done | bytes 4128 | tf_op jit(solution)/shard_map/ppermute | solution.py:265
  17.1 8.3 %all_to_all.17 = f32[16,2,128]{2,1,0:T(2,128)S(1)} all-to-all(f32[16,2,128]{2,1,0:T(2,128)S(1)} %bitcast.6), channel_id=1, replica_groups={{30,12,24,1,6,8,14,26,20,16,4,18,22,28,10,2},{31,13,25,0,7,9,15,27,21,1..., dimensions={0} | all-to-all | bytes 32768 | tf_op jit(solution)/shard_map/all_to_all | solution.py:348
  25.4 0.7 %shard_map.73 = f32[1,32]{1,0:T(1,128)} custom-call(f32[32,128]{1,0:T(8,128)S(1)} %bitcast.7), custom_call_target="tpu_custom_call" | custom-call | tf_op jit(solution)/shard_map/pallas_call | solution.py:356
  (1 shorter events, 0.0 us)
Async XLA Ops:
  0.6 1.9 %collective-permute-start = (bf16[32,4096]{1,0:T(8,128)(2,1)}, bf16[32,4096]{1,0:T(8,128)(2,1)S(1)}, u32[]{:S(2)}, u32[]{:S(2)}) collective-permute-start(bf16[32,4096]{1,0:T(8,128)(2,1)} %own_hbm.1), channel_id=1, source_target_pairs={{1,0},{0,1},{3,2},{2,3},{5,4},{4,5},{7,6},{6,7},{9,8},{8,9},{11,10... | collective-permute-start | bytes 786440 | tf_op jit(solution)/shard_map/ppermute | solution.py:265
  15.9 1.2 %collective-permute-start.1 = (f32[8,128]{1,0:T(8,128)S(1)}, f32[8,128]{1,0:T(8,128)S(1)}, u32[]{:S(2)}, u32[]{:S(2)}) collective-permute-start(f32[8,128]{1,0:T(8,128)S(1)} %get-tuple-element.19.refs_0_), channel_id=1, source_target_pairs={{1,0},{0,1},{3,2},{2,3},{5,4},{4,5},{7,6},{6,7},{9,8},{8,9},{11,10... | collective-permute-start | bytes 12296 | tf_op jit(solution)/shard_map/ppermute | solution.py:265

commit v9 on v8

--- a/solution.py
+++ b/solution.py
@@ -204,20 +204,29 @@
     out_ref[...] = from_first(scores_ref[...], lax.axis_index("qry"), rows_dev, query_groups)
 
 
-def spread_kernel(first_place, *refs):
+def joined(parts, rows_dev):
+    peak = functools.reduce(jnp.maximum, parts)
+    weights = [jnp.exp(part - peak) for part in parts]
+    total = functools.reduce(jnp.add, weights)
+    moved = [rolled(weight, weight.shape[1] - rows_dev) for weight in weights + [total]]
+    weighted = functools.reduce(jnp.add, [w * part for w, part in zip(moved, parts)])
+    lane = lax.broadcasted_iota(jnp.int32, peak.shape, 1)
+    totals = peak + jnp.log(total)
+    return jnp.where(lane < 2 * rows_dev, totals, weighted / moved[-1])
+
+
+def spread_kernel(first_place, rows_dev, *refs):
     line_refs, out_ref = refs[:-1], refs[-1]
     sources = len(line_refs)
-    row = lax.broadcasted_iota(jnp.int32, out_ref.shape, 0)
-    source = row % sources
-    crossed = jnp.where(row // sources == first_place, 1, 0)
+    place = lax.broadcasted_iota(jnp.int32, out_ref.shape, 0)
+    crossed = jnp.where(place == first_place, 1, 0)
     here = jnp.where(lax.axis_index("doc") == 0, 1, 0)
     part = (crossed - here + sources) % sources
     out = jnp.zeros(out_ref.shape, jnp.float32)
-    for k, lines in enumerate(line_refs):
-        for ahead in range(sources):
-            held = (ahead - k) % sources
-            line = jnp.broadcast_to(lines[held : held + 1, :], out_ref.shape)
-            out = jnp.where((source == k) & (part == ahead), line, out)
+    for ahead in range(sources):
+        held = [(ahead - k) % sources for k in range(sources)]
+        line = joined([lines[h : h + 1, :] for lines, h in zip(line_refs, held)], rows_dev)
+        out = jnp.where(part == ahead, jnp.broadcast_to(line, out_ref.shape), out)
     out_ref[...] = out
 
 
@@ -270,7 +279,6 @@
 def on_device(queries, passages, passage_route, pattern, teacher):
     doc_count = lax.axis_size("doc")
     query_groups = lax.axis_size("qry")
-    devices = doc_count * query_groups
     rows_dev, width = queries.shape
     rows = passages.shape[0]
     all_queries, doc_dev = teacher.shape
@@ -341,8 +349,8 @@
     )(doc_scores)
     doc_scores, received = lax.optimization_barrier((doc_scores, received))
     partials = call(
-        functools.partial(spread_kernel, order.index(0)),
-        shaped((devices, line), f32),
+        functools.partial(spread_kernel, order.index(0), rows_dev),
+        shaped((doc_count, line), f32),
         [VMEM] * query_groups,
     )(lines, *received)
     everyone = lax.all_to_all(

time: 26.4 us -> 26.3 us (level)
  no operation moved by 1% of the time
where the time goes in v9:
time: 26.3 us; the launch traced here: 26 us
  blocking collectives  20.4 us (78%)
  Pallas kernels  3.92 us (15%)
  between operations  0.67 us (3%)
  starting transfers between devices  0.53 us (2%)
  waiting for transfers between devices  0.48 us (2%)
    all_to_all x1, blocking collectives, on_device(): lax.all_to_all(outgoing, 'doc', split_axis=0, concat_axis=0, axis_index_g...  12.2 us
    all_to_all x1, blocking collectives, on_device(): lax.all_to_all(partials, ('doc', 'qry'), split_axis=0, concat_axis=0, axi...  8.19 us
    pallas_call x1, Pallas kernels, on_device(): call(functools.partial(before_kernel, (doc_count, query_groups, capacity,...  1.38 us
    pallas_call x1, Pallas kernels, on_device(): call(pack_kernel, shaped((doc_count, capacity + SUBLANES, 2 * all_queries...  0.74 us
    pallas_call x1, Pallas kernels, on_device(): call(functools.partial(merge_kernel, rows_dev), shaped((1, rows_dev), f32...  0.68 us
    pallas_call x1, Pallas kernels, on_device(): call(functools.partial(order_kernel, rows_dev, query_groups), shaped((doc...  0.67 us
    ppermute x2, starting transfers between devices, from_others(): lax.ppermute(array, 'qry', [((i + k) % query_groups, i) for i in range(qu...  0.53 us
  transfers between devices with their start and end apart: 2, of which 1 were waited for; matrix products, arithmetic and copies ran while one was open for 0% of the time, Pallas kernels for 8%

profile of v9, /device:TPU:0, one launch (start us, length us, event | category | flops | bytes accessed | tf_op | source)
XLA Modules:
  0.0 26.0 jit_solution(6000652946526847197)
XLA Ops:
  0.6 0.5 %collective-permute-start = (bf16[32,4096]{1,0:T(8,128)(2,1)}, bf16[32,4096]{1,0:T(8,128)(2,1)S(1)}, u32[]{:S(2)}, u32[]{:S(2)}) collective-permute-start(bf16[32,4096]{1,0:T(8,128)(2,1)} %own_hbm.1), channel_id=1, source_target_pairs={{1,0},{0,1},{3,2},{2,3},{5,4},{4,5},{7,6},{6,7},{9,8},{8,9},{11,10... | collective-permute-start | bytes 786440 | tf_op jit(solution)/shard_map/ppermute | solution.py:274
  1.1 1.4 %shard_map.68 = (bf16[136,4096]{1,0:T(8,128)(2,1)S(1)}, bf16[32,4096]{1,0:T(8,128)(2,1)S(1)}, bf16[256,136]{1,0:T(8,128)(2,1)S(1)}, f32[128,128]{1,0:T(8,128)S(1...) custom-call(bf16[136,4096]{1,0:T(8,128)(2,1)} %passages_hbm.1, bf16[32,4096]{1,0:T(8,128)(2,1)} %own_hbm.1, ...), custom_call_target="tpu_custom_call" | custom-call | flops 34816 | bytes 1376256 | tf_op jit(solution)/shard_map/pallas_call | solution.py:294
  2.5 0.0 collective-permute-done.refs_1_
  2.5 0.7 %shard_map.69 = bf16[16,24,128]{2,1,0:T(8,128)(2,1)S(1)} custom-call(bf16[136,4096]{1,0:T(8,128)(2,1)S(1)} %get-tuple-element.12.passages_ref, bf16[256,136]{1,0:T(8,128)(2,1)S(1)} %get-tuple-element.13.place_ref, f32[128,128]{1,0:T(8,128)S(1)} %get-tuple-element.14.ids_ref, bf16[32,4096]{1,0:T(8,128)(2,1)S(1)} %get-tuple-element.15.refs_0_, ...), custom_call_target="tpu_custom_call" | custom-call | tf_op jit(solution)/shard_map/pallas_call | solution.py:324
  3.3 12.2 %all_to_all.16.arrived_ref = bf16[16,24,128]{2,1,0:T(8,128)(2,1)S(1)} all-to-all(bf16[16,24,128]{2,1,0:T(8,128)(2,1)S(1)} %shard_map.69), channel_id=1, replica_groups={{22,12,26,0,6,8,14,28,20,16,4,18,24,30,10,2},{23,13,27,1,7,9,15,29,21,1..., dimensions={0} | all-to-all | bytes 196608 | tf_op jit(solution)/shard_map/all_to_all | solution.py:329
  15.5 0.4 %shard_map.70 = (f32[16,64]{1,0:T(8,128)S(1)}, f32[8,128]{1,0:T(8,128)S(1)}) custom-call(bf16[16,24,128]{2,1,0:T(8,128)(2,1)S(1)} %all_to_all.16.arrived_ref, f32[16,64]{1,0:T(8,128)S(1)} %get-tuple-element.16.weights_ref, f32[8,64]{1,0:T(8,128)S(1)} %get-tuple-element.17.notes_ref), custom_call_target="tpu_custom_call" | custom-call | tf_op jit(solution)/shard_map/pallas_call | solution.py:339
  15.9 0.0 collective-permute-start.1
  15.9 0.7 %shard_map.71 = f32[16,64]{1,0:T(8,128)} custom-call(f32[16,64]{1,0:T(8,128)S(1)} %get-tuple-element.18.scores_ref), custom_call_target="tpu_custom_call" | custom-call | tf_op jit(solution)/shard_map/pallas_call | solution.py:345
  16.6 0.5 %collective-permute-done.1.refs_1_ = f32[8,128]{1,0:T(8,128)S(1)} collective-permute-done((f32[8,128]{1,0:T(8,128)S(1)}, f32[8,128]{1,0:T(8,128)S(1)}, u32[]{:S(2)}, u32[]{:S(2)}) %collective-permute-start.1) | collective-permute-done | bytes 4128 | tf_op jit(solution)/shard_map/ppermute | solution.py:274
  17.1 0.1 shard_map.72
  17.1 8.2 %all_to_all.17 = f32[16,1,128]{2,1,0:T(1,128)S(1)} all-to-all(f32[16,1,128]{2,1,0:T(1,128)S(1)} %bitcast.8), channel_id=1, replica_groups={{30,12,24,1,6,8,14,26,20,16,4,18,22,28,10,2},{31,13,25,0,7,9,15,27,21,1..., dimensions={0} | all-to-all | bytes 16384 | tf_op jit(solution)/shard_map/all_to_all | solution.py:356
  25.3 0.7 %shard_map.73 = f32[1,32]{1,0:T(1,128)} custom-call(f32[16,128]{1,0:T(8,128)S(1)} %bitcast.9), custom_call_target="tpu_custom_call" | custom-call | tf_op jit(solution)/shard_map/pallas_call | solution.py:364
Async XLA Ops:
  0.6 1.9 %collective-permute-start = (bf16[32,4096]{1,0:T(8,128)(2,1)}, bf16[32,4096]{1,0:T(8,128)(2,1)S(1)}, u32[]{:S(2)}, u32[]{:S(2)}) collective-permute-start(bf16[32,4096]{1,0:T(8,128)(2,1)} %own_hbm.1), channel_id=1, source_target_pairs={{1,0},{0,1},{3,2},{2,3},{5,4},{4,5},{7,6},{6,7},{9,8},{8,9},{11,10... | collective-permute-start | bytes 786440 | tf_op jit(solution)/shard_map/ppermute | solution.py:274
  15.9 1.2 %collective-permute-start.1 = (f32[8,128]{1,0:T(8,128)S(1)}, f32[8,128]{1,0:T(8,128)S(1)}, u32[]{:S(2)}, u32[]{:S(2)}) collective-permute-start(f32[8,128]{1,0:T(8,128)S(1)} %get-tuple-element.19.refs_0_), channel_id=1, source_target_pairs={{1,0},{0,1},{3,2},{2,3},{5,4},{4,5},{7,6},{6,7},{9,8},{8,9},{11,10... | collective-permute-start | bytes 12296 | tf_op jit(solution)/shard_map/ppermute | solution.py:274

commit v10 on v9

--- a/solution.py
+++ b/solution.py
@@ -94,7 +94,7 @@
     position = jnp.sum(jnp.where(earlier, 1.0, 0.0), axis=0, keepdims=True)
     placing = target * capacity + position
     outgoing = lax.broadcasted_iota(jnp.int32, (doc_count * capacity, rows), 0).astype(jnp.float32)
-    place_ref[...] = jnp.where(outgoing == placing, 1.0, 0.0).astype(place_ref.dtype)
+    place_ref[...] = jnp.where(outgoing == placing, score_scale, 0.0).astype(place_ref.dtype)
     columns = ids_ref.shape[1]
     mine = place_in(order, jnp.full((1, 1), lax.axis_index("doc"), jnp.int32)) * capacity
     arriving = as_column(position) + mine.astype(jnp.float32)
@@ -140,7 +140,7 @@
     doc_count, block_rows, columns = out_ref.shape
     capacity = block_rows - SUBLANES
     queries = jnp.concatenate([part[...] for part in query_refs], axis=0)
-    logits = dot_nt(passages_ref[...], queries) * score_scale
+    logits = dot_nt(passages_ref[...], queries)
     high = logits.astype(jnp.bfloat16)
     low = (logits - high.astype(jnp.float32)).astype(jnp.bfloat16)
     placed = jnp.dot(

time: 26.3 us -> 26.3 us (level)
  no operation moved by 1% of the time
where the time goes in v10:
time: 26.3 us; the launch traced here: 26 us
  blocking collectives  20.4 us (78%)
  Pallas kernels  3.92 us (15%)
  between operations  0.67 us (3%)
  starting transfers between devices  0.53 us (2%)
  waiting for transfers between devices  0.48 us (2%)
    all_to_all x1, blocking collectives, on_device(): lax.all_to_all(outgoing, 'doc', split_axis=0, concat_axis=0, axis_index_g...  12.2 us
    all_to_all x1, blocking collectives, on_device(): lax.all_to_all(partials, ('doc', 'qry'), split_axis=0, concat_axis=0, axi...  8.19 us
    pallas_call x1, Pallas kernels, on_device(): call(functools.partial(before_kernel, (doc_count, query_groups, capacity,...  1.38 us
    pallas_call x1, Pallas kernels, on_device(): call(pack_kernel, shaped((doc_count, capacity + SUBLANES, 2 * all_queries...  0.74 us
    pallas_call x1, Pallas kernels, on_device(): call(functools.partial(merge_kernel, rows_dev), shaped((1, rows_dev), f32...  0.68 us
    pallas_call x1, Pallas kernels, on_device(): call(functools.partial(order_kernel, rows_dev, query_groups), shaped((doc...  0.67 us
    ppermute x2, starting transfers between devices, from_others(): lax.ppermute(array, 'qry', [((i + k) % query_groups, i) for i in range(qu...  0.53 us
  transfers between devices with their start and end apart: 2, of which 1 were waited for; matrix products, arithmetic and copies ran while one was open for 0% of the time, Pallas kernels for 8%

profile of v10, /device:TPU:0, one launch (start us, length us, event | category | flops | bytes accessed | tf_op | source)
XLA Modules:
  0.0 26.0 jit_solution(7700559142569853610)
XLA Ops:
  0.6 0.5 %collective-permute-start = (bf16[32,4096]{1,0:T(8,128)(2,1)}, bf16[32,4096]{1,0:T(8,128)(2,1)S(1)}, u32[]{:S(2)}, u32[]{:S(2)}) collective-permute-start(bf16[32,4096]{1,0:T(8,128)(2,1)} %own_hbm.1), channel_id=1, source_target_pairs={{1,0},{0,1},{3,2},{2,3},{5,4},{4,5},{7,6},{6,7},{9,8},{8,9},{11,10... | collective-permute-start | bytes 786440 | tf_op jit(solution)/shard_map/ppermute | solution.py:274
  1.1 1.4 %shard_map.68 = (bf16[136,4096]{1,0:T(8,128)(2,1)S(1)}, bf16[32,4096]{1,0:T(8,128)(2,1)S(1)}, bf16[256,136]{1,0:T(8,128)(2,1)S(1)}, f32[128,128]{1,0:T(8,128)S(1...) custom-call(bf16[136,4096]{1,0:T(8,128)(2,1)} %passages_hbm.1, bf16[32,4096]{1,0:T(8,128)(2,1)} %own_hbm.1, ...), custom_call_target="tpu_custom_call" | custom-call | flops 34816 | bytes 1376256 | tf_op jit(solution)/shard_map/pallas_call | solution.py:294
  2.5 0.0 collective-permute-done.refs_1_
  2.5 0.7 %shard_map.69 = bf16[16,24,128]{2,1,0:T(8,128)(2,1)S(1)} custom-call(bf16[136,4096]{1,0:T(8,128)(2,1)S(1)} %get-tuple-element.12.passages_ref, bf16[256,136]{1,0:T(8,128)(2,1)S(1)} %get-tuple-element.13.place_ref, f32[128,128]{1,0:T(8,128)S(1)} %get-tuple-element.14.ids_ref, bf16[32,4096]{1,0:T(8,128)(2,1)S(1)} %get-tuple-element.15.refs_0_, ...), custom_call_target="tpu_custom_call" | custom-call | tf_op jit(solution)/shard_map/pallas_call | solution.py:324
  3.3 12.2 %all_to_all.16.arrived_ref = bf16[16,24,128]{2,1,0:T(8,128)(2,1)S(1)} all-to-all(bf16[16,24,128]{2,1,0:T(8,128)(2,1)S(1)} %shard_map.69), channel_id=1, replica_groups={{22,12,26,0,6,8,14,28,20,16,4,18,24,30,10,2},{23,13,27,1,7,9,15,29,21,1..., dimensions={0} | all-to-all | bytes 196608 | tf_op jit(solution)/shard_map/all_to_all | solution.py:329
  15.5 0.4 %shard_map.70 = (f32[16,64]{1,0:T(8,128)S(1)}, f32[8,128]{1,0:T(8,128)S(1)}) custom-call(bf16[16,24,128]{2,1,0:T(8,128)(2,1)S(1)} %all_to_all.16.arrived_ref, f32[16,64]{1,0:T(8,128)S(1)} %get-tuple-element.16.weights_ref, f32[8,64]{1,0:T(8,128)S(1)} %get-tuple-element.17.notes_ref), custom_call_target="tpu_custom_call" | custom-call | tf_op jit(solution)/shard_map/pallas_call | solution.py:339
  15.9 0.0 collective-permute-start.1
  15.9 0.7 %shard_map.71 = f32[16,64]{1,0:T(8,128)} custom-call(f32[16,64]{1,0:T(8,128)S(1)} %get-tuple-element.18.scores_ref), custom_call_target="tpu_custom_call" | custom-call | tf_op jit(solution)/shard_map/pallas_call | solution.py:345
  16.6 0.5 %collective-permute-done.1.refs_1_ = f32[8,128]{1,0:T(8,128)S(1)} collective-permute-done((f32[8,128]{1,0:T(8,128)S(1)}, f32[8,128]{1,0:T(8,128)S(1)}, u32[]{:S(2)}, u32[]{:S(2)}) %collective-permute-start.1) | collective-permute-done | bytes 4128 | tf_op jit(solution)/shard_map/ppermute | solution.py:274
  17.1 0.1 shard_map.72
  17.1 8.2 %all_to_all.17 = f32[16,1,128]{2,1,0:T(1,128)S(1)} all-to-all(f32[16,1,128]{2,1,0:T(1,128)S(1)} %bitcast.8), channel_id=1, replica_groups={{30,12,24,1,6,8,14,26,20,16,4,18,22,28,10,2},{31,13,25,0,7,9,15,27,21,1..., dimensions={0} | all-to-all | bytes 16384 | tf_op jit(solution)/shard_map/all_to_all | solution.py:356
  25.3 0.7 %shard_map.73 = f32[1,32]{1,0:T(1,128)} custom-call(f32[16,128]{1,0:T(8,128)S(1)} %bitcast.9), custom_call_target="tpu_custom_call" | custom-call | tf_op jit(solution)/shard_map/pallas_call | solution.py:364
Async XLA Ops:
  0.6 1.9 %collective-permute-start = (bf16[32,4096]{1,0:T(8,128)(2,1)}, bf16[32,4096]{1,0:T(8,128)(2,1)S(1)}, u32[]{:S(2)}, u32[]{:S(2)}) collective-permute-start(bf16[32,4096]{1,0:T(8,128)(2,1)} %own_hbm.1), channel_id=1, source_target_pairs={{1,0},{0,1},{3,2},{2,3},{5,4},{4,5},{7,6},{6,7},{9,8},{8,9},{11,10... | collective-permute-start | bytes 786440 | tf_op jit(solution)/shard_map/ppermute | solution.py:274
  15.9 1.2 %collective-permute-start.1 = (f32[8,128]{1,0:T(8,128)S(1)}, f32[8,128]{1,0:T(8,128)S(1)}, u32[]{:S(2)}, u32[]{:S(2)}) collective-permute-start(f32[8,128]{1,0:T(8,128)S(1)} %get-tuple-element.19.refs_0_), channel_id=1, source_target_pairs={{1,0},{0,1},{3,2},{2,3},{5,4},{4,5},{7,6},{6,7},{9,8},{8,9},{11,10... | collective-permute-start | bytes 12296 | tf_op jit(solution)/shard_map/ppermute | solution.py:274

commit v11 on v9

--- a/solution.py
+++ b/solution.py
@@ -13,6 +13,7 @@
 SUBLANES = 8
 PACKED = 16
 ORDER_SEED = 25
+TOTALS_SEED = 35
 
 score_scale = 0.03125
 very_negative = -1e30
@@ -264,9 +265,9 @@
     ]
 
 
-def shuffled_from(first, size):
+def shuffled_from(first, size, seed=ORDER_SEED):
     others = [k for k in range(size) if k != first]
-    return [first] + random.Random(ORDER_SEED).sample(others, size - 1)
+    return [first] + random.Random(seed).sample(others, size - 1)
 
 
 def from_others(array, query_groups):
@@ -285,7 +286,7 @@
     table_rows = doc_dev * MAXP
     capacity = -(-table_rows // (doc_count * PACKED)) * PACKED
     last_doc = doc_count - 1
-    order = shuffled_from(last_doc, doc_count)
+    order = shuffled_from(last_doc, doc_count, TOTALS_SEED)
     route_order = shuffled_from(last_doc - doc_count // 4, doc_count)
     f32, bf16 = jnp.float32, jnp.bfloat16
     shaped = jax.ShapeDtypeStruct

time: 26.3 us -> 26.3 us (level)
  no operation moved by 1% of the time
where the time goes in v11:
time: 26.3 us; the launch traced here: 26 us
  blocking collectives  20.4 us (78%)
  Pallas kernels  3.92 us (15%)
  between operations  0.67 us (3%)
  starting transfers between devices  0.53 us (2%)
  waiting for transfers between devices  0.48 us (2%)
    all_to_all x1, blocking collectives, on_device(): lax.all_to_all(outgoing, 'doc', split_axis=0, concat_axis=0, axis_index_g...  12.2 us
    all_to_all x1, blocking collectives, on_device(): lax.all_to_all(partials, ('doc', 'qry'), split_axis=0, concat_axis=0, axi...  8.18 us
    pallas_call x1, Pallas kernels, on_device(): call(functools.partial(before_kernel, (doc_count, query_groups, capacity,...  1.38 us
    pallas_call x1, Pallas kernels, on_device(): call(pack_kernel, shaped((doc_count, capacity + SUBLANES, 2 * all_queries...  0.74 us
    pallas_call x1, Pallas kernels, on_device(): call(functools.partial(merge_kernel, rows_dev), shaped((1, rows_dev), f32...  0.68 us
    pallas_call x1, Pallas kernels, on_device(): call(functools.partial(order_kernel, rows_dev, query_groups), shaped((doc...  0.67 us
    ppermute x2, starting transfers between devices, from_others(): lax.ppermute(array, 'qry', [((i + k) % query_groups, i) for i in range(qu...  0.53 us
  transfers between devices with their start and end apart: 2, of which 1 were waited for; matrix products, arithmetic and copies ran while one was open for 0% of the time, Pallas kernels for 8%

profile of v11, /device:TPU:0, one launch (start us, length us, event | category | flops | bytes accessed | tf_op | source)
XLA Modules:
  0.0 26.0 jit_solution(1964774887070090138)
XLA Ops:
  0.6 0.5 %collective-permute-start = (bf16[32,4096]{1,0:T(8,128)(2,1)}, bf16[32,4096]{1,0:T(8,128)(2,1)S(1)}, u32[]{:S(2)}, u32[]{:S(2)}) collective-permute-start(bf16[32,4096]{1,0:T(8,128)(2,1)} %own_hbm.1), channel_id=1, source_target_pairs={{1,0},{0,1},{3,2},{2,3},{5,4},{4,5},{7,6},{6,7},{9,8},{8,9},{11,10... | collective-permute-start | bytes 786440 | tf_op jit(solution)/shard_map/ppermute | solution.py:275
  1.1 1.4 %shard_map.68 = (bf16[136,4096]{1,0:T(8,128)(2,1)S(1)}, bf16[32,4096]{1,0:T(8,128)(2,1)S(1)}, bf16[256,136]{1,0:T(8,128)(2,1)S(1)}, f32[128,128]{1,0:T(8,128)S(1...) custom-call(bf16[136,4096]{1,0:T(8,128)(2,1)} %passages_hbm.1, bf16[32,4096]{1,0:T(8,128)(2,1)} %own_hbm.1, ...), custom_call_target="tpu_custom_call" | custom-call | flops 34816 | bytes 1376256 | tf_op jit(solution)/shard_map/pallas_call | solution.py:295
  2.5 0.0 collective-permute-done.refs_1_
  2.5 0.7 %shard_map.69 = bf16[16,24,128]{2,1,0:T(8,128)(2,1)S(1)} custom-call(bf16[136,4096]{1,0:T(8,128)(2,1)S(1)} %get-tuple-element.12.passages_ref, bf16[256,136]{1,0:T(8,128)(2,1)S(1)} %get-tuple-element.13.place_ref, f32[128,128]{1,0:T(8,128)S(1)} %get-tuple-element.14.ids_ref, bf16[32,4096]{1,0:T(8,128)(2,1)S(1)} %get-tuple-element.15.refs_0_, ...), custom_call_target="tpu_custom_call" | custom-call | tf_op jit(solution)/shard_map/pallas_call | solution.py:325
  3.3 12.2 %all_to_all.16.arrived_ref = bf16[16,24,128]{2,1,0:T(8,128)(2,1)S(1)} all-to-all(bf16[16,24,128]{2,1,0:T(8,128)(2,1)S(1)} %shard_map.69), channel_id=1, replica_groups={{22,12,26,0,6,8,14,28,20,16,4,18,24,30,10,2},{23,13,27,1,7,9,15,29,21,1..., dimensions={0} | all-to-all | bytes 196608 | tf_op jit(solution)/shard_map/all_to_all | solution.py:330
  15.5 0.4 %shard_map.70 = (f32[16,64]{1,0:T(8,128)S(1)}, f32[8,128]{1,0:T(8,128)S(1)}) custom-call(bf16[16,24,128]{2,1,0:T(8,128)(2,1)S(1)} %all_to_all.16.arrived_ref, f32[16,64]{1,0:T(8,128)S(1)} %get-tuple-element.16.weights_ref, f32[8,64]{1,0:T(8,128)S(1)} %get-tuple-element.17.notes_ref), custom_call_target="tpu_custom_call" | custom-call | tf_op jit(solution)/shard_map/pallas_call | solution.py:340
  15.9 0.0 collective-permute-start.1
  15.9 0.7 %shard_map.71 = f32[16,64]{1,0:T(8,128)} custom-call(f32[16,64]{1,0:T(8,128)S(1)} %get-tuple-element.18.scores_ref), custom_call_target="tpu_custom_call" | custom-call | tf_op jit(solution)/shard_map/pallas_call | solution.py:346
  16.6 0.5 %collective-permute-done.1.refs_1_ = f32[8,128]{1,0:T(8,128)S(1)} collective-permute-done((f32[8,128]{1,0:T(8,128)S(1)}, f32[8,128]{1,0:T(8,128)S(1)}, u32[]{:S(2)}, u32[]{:S(2)}) %collective-permute-start.1) | collective-permute-done | bytes 4128 | tf_op jit(solution)/shard_map/ppermute | solution.py:275
  17.1 0.1 shard_map.72
  17.1 8.2 %all_to_all.17 = f32[16,1,128]{2,1,0:T(1,128)S(1)} all-to-all(f32[16,1,128]{2,1,0:T(1,128)S(1)} %bitcast.8), channel_id=1, replica_groups={{30,16,10,24,4,26,22,8,12,18,28,1,14,6,2,20},{31,17,11,25,5,27,23,9,13,..., dimensions={0} | all-to-all | bytes 16384 | tf_op jit(solution)/shard_map/all_to_all | solution.py:357
  25.3 0.7 %shard_map.73 = f32[1,32]{1,0:T(1,128)} custom-call(f32[16,128]{1,0:T(8,128)S(1)} %bitcast.9), custom_call_target="tpu_custom_call" | custom-call | tf_op jit(solution)/shard_map/pallas_call | solution.py:365
Async XLA Ops:
  0.6 1.9 %collective-permute-start = (bf16[32,4096]{1,0:T(8,128)(2,1)}, bf16[32,4096]{1,0:T(8,128)(2,1)S(1)}, u32[]{:S(2)}, u32[]{:S(2)}) collective-permute-start(bf16[32,4096]{1,0:T(8,128)(2,1)} %own_hbm.1), channel_id=1, source_target_pairs={{1,0},{0,1},{3,2},{2,3},{5,4},{4,5},{7,6},{6,7},{9,8},{8,9},{11,10... | collective-permute-start | bytes 786440 | tf_op jit(solution)/shard_map/ppermute | solution.py:275
  15.9 1.2 %collective-permute-start.1 = (f32[8,128]{1,0:T(8,128)S(1)}, f32[8,128]{1,0:T(8,128)S(1)}, u32[]{:S(2)}, u32[]{:S(2)}) collective-permute-start(f32[8,128]{1,0:T(8,128)S(1)} %get-tuple-element.19.refs_0_), channel_id=1, source_target_pairs={{1,0},{0,1},{3,2},{2,3},{5,4},{4,5},{7,6},{6,7},{9,8},{8,9},{11,10... | collective-permute-start | bytes 12296 | tf_op jit(solution)/shard_map/ppermute | solution.py:275
